TPU v7x, 128 devices: a whole 4x4x4 slice. The times are simulated.
128 devices in a mesh: grp: 2 (over core), dp: 32 (over x_hi, z, y), mp: 2 (over x_lo).
Axes of the slice: x: 4 (x_hi: 2, x_lo: 2; x = x_hi * 2 + x_lo), y: 4, z: 4, core: 2. Of those that a mesh axis runs over, the one named last changes fastest.
Arguments:
- hidden_in: bfloat16 [2, 8192, 2048], P('grp', 'dp'), may hold values from -6 to 6
- norm_gain: bfloat16 [2, 2048], P('grp'), may hold values from 0.099609375 to 1.8984375
- router: bfloat16 [2, 2048, 32], P('grp'), may hold values from -0.125 to 0.125
- routes: int32 [2, 8192, 2], P('grp', 'dp'), may hold values from 0 to 31, all different within a row; in each aligned block of 256 rows (0 to 255, 256 to 511, ..., all dimensions but the last counted through in order) at most 32 rows name the same one
- expert_in: bfloat16 [2, 32, 2048, 4096], P('grp', 'dp', None, 'mp'), may hold values from -0.125 to 0.125
- expert_out: bfloat16 [2, 32, 4096, 2048], P('grp', 'dp', 'mp'), may hold values from -0.09375 to 0.09375
- attn_weight: bfloat16 [2, 2, 2048, 1024], P('grp', None, None, 'mp'), may hold values from -0.125 to 0.125
- src_segments: int32 [32, 256], P('dp'), may hold values from 0 to 7, never falling along the last dimension, each value on 1 to 128 neighbouring positions
- tgt_segments: int32 [32, 256], P('dp'), may hold values from 0 to 7, never falling along the last dimension, each value on 1 to 128 neighbouring positions
- cotangent: bfloat16 [8192, 2048], P('dp'), may hold values from -6 to 6
Outputs:
- layer_out: bfloat16 [2, 8192, 2048], P('grp', 'dp', 'mp')
- input_grad: bfloat16 [2, 8192, 2048], P('grp', 'dp', 'mp')
Inputs may be any that keep to these rules, and one draw needn't show every extreme that they name: `routes`: each row names two different experts. Within the 256 rows of one batch row of one group no expert is named by more than 32 rows, and in every draw some expert is named by exactly 32 rows of some batch row. `src_segments`: in each row the numbers never fall, and each of the 8 sentences holds 1 to 128 positions, one exactly 128. `tgt_segments`: in each row the numbers never fall, and each of the 8 sentences holds 1 to 128 positions, one exactly 128.
All inputs are finite; a program needn't handle non-finite values.
Results may differ from a plain program's by a relative error of at most 0.019.
Values may be sent and summed in bfloat16 or wider, within the bound.
A program may use at most 128 MiB of HBM per device.

v0:
```python
import jax
import jax.numpy as jnp
from jax import lax
from jax.sharding import PartitionSpec as P

HEAD_DIM = 128


def passed_along(value, axis, by):
    peers = lax.axis_size(axis)
    pairs = [(i, i + by) for i in range(peers) if 0 <= i + by < peers]
    return lax.ppermute(value, axis, pairs)


def layer_norm(token_rows, gain_row):
    values = token_rows.astype(jnp.float32)
    centred = values - jnp.mean(values, -1, keepdims=True)
    variance = jnp.mean(centred * centred, -1, keepdims=True)
    return (centred * lax.rsqrt(variance + 1e-05) * gain_row.astype(jnp.float32)).astype(
        jnp.bfloat16
    )


def gate_pairs(normed, router_matrix, route_rows):
    logits = jnp.dot(normed, router_matrix, preferred_element_type=jnp.float32)
    expert_ids = jnp.arange(logits.shape[1], dtype=jnp.int32)
    chosen = jnp.sum(
        jnp.where(
            route_rows[:, :, None] == expert_ids[None, None, :],
            logits[:, None, :],
            jnp.zeros((), logits.dtype),
        ),
        -1,
    )
    leading = jax.nn.sigmoid(chosen[:, 0] - chosen[:, 1])
    return jnp.stack([leading, 1.0 - leading], 1)


def slot_layout(route_rows, expert_count, capacity):
    token_count = route_rows.shape[0]
    flat_ids = route_rows.reshape(-1)
    onehot = (flat_ids[:, None] == jnp.arange(expert_count, dtype=jnp.int32)[None, :]).astype(
        jnp.int32
    )
    earlier = jnp.cumsum(onehot, 0) - onehot
    slot_rank = jnp.sum(earlier * onehot, 1)
    slot_index = flat_ids * capacity + slot_rank
    pair_token = jnp.arange(2 * token_count, dtype=jnp.int32) // 2
    slot_owner = (
        jnp.full((expert_count * capacity,), token_count, jnp.int32).at[slot_index].set(pair_token)
    )
    return (slot_index, slot_owner)


def contract_rows(left_rows, weight):
    return lax.dot_general(
        left_rows, weight, (((1,), (1,)), ((), ())), preferred_element_type=jnp.float32
    )


def cross_attend(query_rows, key_rows, value_rows, seg_mask, cot_rows, query_weight, out_weight):
    token_count = query_rows.shape[0]
    source_count = key_rows.shape[0]
    head_count = query_rows.shape[1] // HEAD_DIM
    softmax_scale = HEAD_DIM ** (-0.5)
    query_heads = query_rows.reshape(token_count, head_count, HEAD_DIM)
    key_heads = key_rows.reshape(source_count, head_count, HEAD_DIM)
    value_heads = value_rows.reshape(source_count, head_count, HEAD_DIM)
    scores = (
        jnp.einsum("qhd,khd->hqk", query_heads, key_heads, preferred_element_type=jnp.float32)
        * softmax_scale
    )
    exp_scores = jnp.exp(scores) * seg_mask[None]
    weights = exp_scores / jnp.sum(exp_scores, -1, keepdims=True)
    weights_b = weights.astype(jnp.bfloat16)
    context = jnp.einsum(
        "hqk,khd->qhd", weights_b, value_heads, preferred_element_type=jnp.float32
    ).astype(jnp.bfloat16)
    out_term = contract_rows(context.reshape(token_count, -1), out_weight)
    context_grad = jnp.dot(cot_rows, out_weight, preferred_element_type=jnp.float32).astype(
        jnp.bfloat16
    )
    grad_heads = context_grad.reshape(token_count, head_count, HEAD_DIM)
    prob_grad = jnp.einsum(
        "qhd,khd->hqk", grad_heads, value_heads, preferred_element_type=jnp.float32
    )
    row_delta = jnp.sum(weights * prob_grad, -1, keepdims=True)
    score_grad = (weights * (prob_grad - row_delta)).astype(jnp.bfloat16)
    query_grad = (
        jnp.einsum("hqk,khd->qhd", score_grad, key_heads, preferred_element_type=jnp.float32)
        * softmax_scale
    ).astype(jnp.bfloat16)
    key_grad = (
        jnp.einsum("hqk,qhd->khd", score_grad, query_heads, preferred_element_type=jnp.float32)
        * softmax_scale
    ).astype(jnp.bfloat16)
    value_grad = jnp.einsum(
        "hqk,qhd->khd", weights_b, grad_heads, preferred_element_type=jnp.float32
    ).astype(jnp.bfloat16)
    query_term = contract_rows(query_grad.reshape(token_count, -1), query_weight)
    key_value_grads = jnp.stack(
        [key_grad.reshape(source_count, -1), value_grad.reshape(source_count, -1)]
    )
    return (out_term, query_term, key_value_grads)


def per_device(
    hidden_in,
    norm_gain,
    router,
    routes,
    expert_in,
    expert_out,
    attn_weight,
    src_segments,
    tgt_segments,
    cotangent,
):
    group_index = lax.axis_index("grp")
    mp_index = lax.axis_index("mp")
    expert_count = lax.axis_size("dp")
    token_rows = hidden_in[0]
    token_count, model_width = token_rows.shape
    capacity = 4 * token_count // expert_count
    half_width = model_width // lax.axis_size("mp")
    normed = layer_norm(token_rows, norm_gain[0])
    route_rows = routes[0]
    gate_rows = gate_pairs(normed, router[0], route_rows)
    slot_index, slot_owner = slot_layout(route_rows, expert_count, capacity)
    weight_in = expert_in[0, 0]
    weight_out = expert_out[0, 0]
    padded = jnp.concatenate([normed, jnp.zeros((1, normed.shape[1]), normed.dtype)], 0)
    outgoing = padded[slot_owner].reshape(expert_count, capacity, normed.shape[1])
    arrived = lax.all_to_all(outgoing, "dp", split_axis=0, concat_axis=0, tiled=True)
    slot_count = arrived.shape[1]
    expert_inner = jax.nn.relu(
        jnp.dot(arrived.reshape(-1, model_width), weight_in, preferred_element_type=jnp.float32)
    ).astype(jnp.bfloat16)
    expert_term = jnp.dot(expert_inner, weight_out, preferred_element_type=jnp.float32)
    summed = lax.psum(expert_term, "mp")
    result_rows = summed.astype(jnp.bfloat16).reshape(arrived.shape[0], slot_count, summed.shape[1])
    returned_rows = lax.all_to_all(result_rows, "dp", split_axis=0, concat_axis=0, tiled=True)
    picked_rows = returned_rows.reshape(expert_count * capacity, -1)[slot_index]
    picked_rows = picked_rows.reshape(token_count, 2, -1).astype(jnp.float32)
    mixed_rows = jnp.sum(gate_rows[:, :, None] * picked_rows, 1)
    layer_state = (token_rows.astype(jnp.float32) + mixed_rows).astype(jnp.bfloat16)
    state_half = lax.dynamic_slice_in_dim(layer_state, mp_index * half_width, half_width, 1)
    proj_first = attn_weight[0, 0]
    proj_second = attn_weight[0, 1]
    projected = jnp.dot(layer_state, proj_first, preferred_element_type=jnp.float32).astype(
        jnp.bfloat16
    )

    def encoder_values():
        return jnp.dot(layer_state, proj_second, preferred_element_type=jnp.float32).astype(
            jnp.bfloat16
        )

    def absent_values():
        return jnp.zeros_like(projected)

    value_rows = lax.cond(group_index == 0, encoder_values, absent_values)
    handed = passed_along(jnp.stack([projected, value_rows]), "grp", 1)
    seg_mask = (tgt_segments[0][:, None] == src_segments[0][None, :]).astype(jnp.float32)

    def decoder_side():
        return cross_attend(
            projected, handed[0], handed[1], seg_mask, cotangent, proj_first, proj_second
        )

    def encoder_side():
        zero_rows = jnp.zeros((token_count, model_width), jnp.float32)
        return (zero_rows, zero_rows, jnp.zeros_like(handed))

    out_term, query_term, key_value_grads = lax.cond(group_index == 1, decoder_side, encoder_side)
    grads_in = passed_along(key_value_grads, "grp", -1)

    def encoder_grad():
        return contract_rows(grads_in[0], proj_first) + contract_rows(grads_in[1], proj_second)

    def decoder_grad():
        return query_term

    grad_term = lax.cond(group_index == 0, encoder_grad, decoder_grad)
    out_share, grad_share = (
        lax.psum_scatter(
            out_term.astype(jnp.bfloat16), "mp", scatter_dimension=1, tiled=True
        ).astype(jnp.float32),
        lax.psum_scatter(
            grad_term.astype(jnp.bfloat16), "mp", scatter_dimension=1, tiled=True
        ).astype(jnp.float32),
    )
    cot_half = lax.dynamic_slice_in_dim(cotangent, mp_index * half_width, half_width, 1)
    forward = jnp.where(
        group_index == 0,
        state_half,
        (state_half.astype(jnp.float32) + out_share).astype(jnp.bfloat16),
    )
    backward = jnp.where(
        group_index == 0,
        grad_share.astype(jnp.bfloat16),
        (cot_half.astype(jnp.float32) + grad_share).astype(jnp.bfloat16),
    )
    return (forward[None], backward[None])


def solution(mesh):
    return jax.shard_map(
        per_device,
        mesh=mesh,
        in_specs=(
            P("grp", "dp", None),
            P("grp", None),
            P("grp", None, None),
            P("grp", "dp", None),
            P("grp", "dp", None, "mp"),
            P("grp", "dp", "mp", None),
            P("grp", None, None, "mp"),
            P("dp", None),
            P("dp", None),
            P("dp", None),
        ),
        out_specs=(P("grp", "dp", "mp"), P("grp", "dp", "mp")),
        check_vma=False,
    )
```

profile of v0, /device:TPU:1, one launch (start us, length us, event | category | flops | bytes accessed | tf_op | source)
XLA Modules:
  0.0 478.5 jit_solution(11715933622705410970)
XLA Ops:
  9.1 1.4 convert_reduce_fusion
  12.9 2.4 scatter_custom_fusion
  15.8 6.0 %gather_fusion = bf16[1024,2048]{1,0:T(8,128)(2,1)} fusion(bf16[257,2048]{1,0:T(8,128)(2,1)S(1)} %concatenate.3, s32[1024]{0:T(1024)S(1)} %fusion.49), kind=kCustom, calls=%fused_computation | custom fusion | bytes 8392704 | tf_op jit(solution)/shard_map/gather | solution.py:133
  21.8 61.4 %all_to_all.10 = bf16[32,32,2048]{2,1,0:T(8,128)(2,1)} all-to-all(bf16[32,32,2048]{2,1,0:T(8,128)(2,1)} %bitcast.138), channel_id=1, replica_groups=mesh['grp'=2,'dp'=32,'mp'=2] {'dp'}, dimensions={0} | all-to-all | bytes 8388608 | tf_op jit(solution)/shard_map/all_to_all | solution.py:134
  83.2 27.6 %fusion.17 = f32[1024,2048]{1,0:T(8,128)} fusion(bf16[1,1,2048,2048]{3,2,1,0:T(8,128)(2,1)} %param.21, bf16[1024,2048]{1,0:T(8,128)(2,1)} %bitcast.139, bf16[1,1,2048,2048]{3,2,1,0:T(8,128)(2,1)} %param.20), kind=kOutput, calls=%fused_computation.31 | convolution fusion | flops 17184063488 | bytes 29360128 | tf_op jit(solution)/shard_map/dot_general | solution.py:139
  110.9 190.9 %all-reduce.2 = bf16[1024,2048]{1,0:T(8,128)(2,1)} all-reduce(f32[1024,2048]{1,0:T(8,128)} %fusion.17), channel_id=1, replica_groups=mesh['grp'=2,'dp'=32,'mp'=2] {'mp'}, use_global_device_ids=true, to_apply=%region_7.8 | all-reduce | flops 2097152 | bytes 12582912 | tf_op jit(solution)/shard_map/psum | solution.py:140
  301.8 9.0 %all-to-all-start.1 = ((bf16[32,32,2048]{2,1,0:T(8,128)(2,1)}), bf16[32,32,2048]{2,1,0:T(8,128)(2,1)}, u32[]{:S(2)}, u32[]{:S(2)}) async-start(bf16[32,32,2048]{2,1,0:T(8,128)(2,1)} %bitcast.137), calls=%async_computation.1 | async-start | bytes 8388608 | tf_op jit(solution)/shard_map/all_to_all | solution.py:142
  311.8 4.5 slice_bitcast_fusion.1
  316.3 41.5 %all-to-all-done.1 = bf16[32,32,2048]{2,1,0:T(8,128)(2,1)} async-done(((bf16[32,32,2048]{2,1,0:T(8,128)(2,1)}), bf16[32,32,2048]{2,1,0:T(8,128)(2,1)}, u32[]{:S(2)}, u32[]{:S(2)}) %all-to-all-start.1) | async-done | bytes 4194336 | tf_op jit(solution)/shard_map/all_to_all | solution.py:142
  357.8 7.1 %gather_fusion.1 = bf16[512,2048]{1,0:T(8,128)(2,1)S(1)} fusion(bf16[1024,2048]{1,0:T(8,128)(2,1)} %bitcast.27, s32[1024]{0:T(1024)S(1)} %pad_clamp_fusion), kind=kCustom, calls=%fused_computation.1 | custom fusion | bytes 4196352 | tf_op jit(solution)/shard_map/gather | solution.py:143
  364.9 4.0 reshape.132
  368.9 8.9 %multiply_reduce_fusion.1 = f32[256,2048]{1,0:T(8,128)S(1)} fusion(f32[256,2,2048]{2,1,0:T(2,128)} %reshape.132, f32[256,2]{1,0:T(8,128)S(1)} %copy.72), kind=kLoop, calls=%fused_computation.36 | loop fusion | flops 1572864 | bytes 6293504 | tf_op jit(solution)/shard_map/reduce_sum | solution.py:145
  378.2 1.8 copy-done.4
  382.7 1.3 collective-permute-start
  384.9 9.5 %collective-permute-done = bf16[2,256,512]{2,1,0:T(8,128)(2,1)S(1)} collective-permute-done((bf16[2,256,512]{2,1,0:T(8,128)(2,1)S(1)}, bf16[2,256,512]{2,1,0:T(8,128)(2,1)S(1)}, u32[]{:S(2)}, u32[]{:S(2)}) %collective-permute-start) | collective-permute-done | bytes 524320 | tf_op jit(solution)/shard_map/ppermute | solution.py:12
  394.4 25.9 %conditional.4 = (bf16[256,2048]{1,0:T(8,128)(2,1)}, bf16[2,256,512]{1,2,0:T(8,128)(2,1)}, bf16[256,2048]{1,0:T(8,128)(2,1)}) conditional(s32[]{:T(128)} %convert_element_type.133, () %tuple.34, (bf16[256,512]{1,0:T(8,128)(2,1)S(1)}, bf16[2,256,512]{2,1,0:T(8,128)(2,1)S(1)}, f32[256,256]{0,1:T(8,128)}, bf16[2048,512]{1,0:T(8,128)(2,1)}, ...), branch_computations={%region_11.12_spmd, %region_12.15_spmd} | conditional | flops 2085227264 | bytes 40116472 | solution.py:175
  395.4 2.6 convolution_convert_fusion.3
  398.9 1.4 fusion.58
  401.6 2.6 multiply_reduce_fusion
  404.2 1.7 multiply_convert_fusion
  406.9 1.4 fusion.2
  408.4 2.7 convolution_convert_fusion.2
  411.1 1.8 pad_maximum_fusion
  413.1 1.7 fusion.59
  414.9 2.0 convolution_convert_fusion.1
  416.9 3.4 fusion.57
  421.6 1.3 collective-permute-start.1
  422.9 1.5 collective-permute-done.1
  424.4 18.7 %reduce-scatter.3.cloned.1.call-done = bf16[256,1024]{1,0:T(8,128)(2,1)} async-done(((bf16[256,2048]{1,0:T(8,128)(2,1)}), bf16[256,1024]{1,0:T(8,128)(2,1)}) %reduce-scatter.3.cloned.1.call-update) | async-done | bytes 524304 | tf_op jit(solution)/shard_map/reduce_scatter | solution.py:186
  443.1 2.0 fusion.43
  445.1 24.2 %reduce-scatter.5.cloned.1.call-done = bf16[256,1024]{1,0:T(8,128)(2,1)} async-done(((bf16[256,2048]{1,0:T(8,128)(2,1)}), bf16[256,1024]{1,0:T(8,128)(2,1)}) %reduce-scatter.5.cloned.1.call-update) | async-done | bytes 524304 | tf_op jit(solution)/shard_map/reduce_scatter | solution.py:189
  469.4 2.3 fusion.42
  (82 shorter events, 15.9 us)
Async XLA Ops:
  7.2 303.9 %copy-start = (bf16[1,2048,32]{1,2,0:T(8,128)(2,1)S(1)}, bf16[1,2048,32]{1,2,0:T(8,128)(2,1)}, u32[]{:S(2)}) copy-start(bf16[1,2048,32]{1,2,0:T(8,128)(2,1)} %param.18) | copy-start | bytes 393220
  7.2 3.4 copy-start.1
  7.2 3.8 copy-start.19
  301.8 56.0 %all-to-all-start.1 = ((bf16[32,32,2048]{2,1,0:T(8,128)(2,1)}), bf16[32,32,2048]{2,1,0:T(8,128)(2,1)}, u32[]{:S(2)}, u32[]{:S(2)}) async-start(bf16[32,32,2048]{2,1,0:T(8,128)(2,1)} %bitcast.137), calls=%async_computation.1 | async-start | bytes 8388608 | tf_op jit(solution)/shard_map/all_to_all | solution.py:142
  310.8 0.8 copy-start.18
  310.8 132.3 %reduce-scatter.3.cloned.1.call-start = ((), (), s32[]{:S(2)}) async-start(), calls=%async_computation.4 | async-start | bytes 1572864 | tf_op jit(solution)/shard_map/reduce_scatter | solution.py:186
  377.8 2.2 copy-start.4
  380.0 1.0 copy-start.8
  380.8 3.3 copy-start.20
  380.8 3.3 copy-start.21
  380.8 13.5 %copy-start.2 = (bf16[2048,512]{1,0:T(8,128)(2,1)S(1)}, bf16[2048,512]{1,0:T(8,128)(2,1)}, u32[]{:S(2)}) copy-start(bf16[2048,512]{1,0:T(8,128)(2,1)} %get-tuple-element.80) | copy-start | bytes 6291460
  382.7 11.6 %collective-permute-start = (bf16[2,256,512]{2,1,0:T(8,128)(2,1)S(1)}, bf16[2,256,512]{2,1,0:T(8,128)(2,1)S(1)}, u32[]{:S(2)}, u32[]{:S(2)}) collective-permute-start(bf16[2,256,512]{2,1,0:T(8,128)(2,1)S(1)} %pad_maximum_fusion.1), channel_id=1, source_target_pairs={{0,64},{1,65},{2,66},{3,67},{4,68},{5,69},{6,70},{7,71},{8,72},{9,... | collective-permute-start | bytes 1572872 | tf_op jit(solution)/shard_map/ppermute | solution.py:12
  394.4 3.7 copy-start.10
  400.3 3.9 copy-start.5
  404.2 2.8 copy-start.6
  404.2 2.8 copy-start.11
  405.9 2.4 copy-start.12
  408.4 2.7 copy-start.14
  408.4 4.5 copy-start.7
  412.9 2.0 copy-start.13
  420.3 49.1 %reduce-scatter.5.cloned.1.call-start = ((), (), s32[]{:S(2)}) async-start(), calls=%async_computation.5 | async-start | bytes 1572864 | tf_op jit(solution)/shard_map/reduce_scatter | solution.py:189
  421.6 2.8 collective-permute-start.1
  424.4 18.7 %copy-start.9 = (bf16[256,2048]{1,0:T(8,128)(2,1)S(1)}, bf16[256,2048]{1,0:T(8,128)(2,1)}, u32[]{:S(2)}) copy-start(bf16[256,2048]{1,0:T(8,128)(2,1)} %copy-done.8) | copy-start | bytes 3145732
  424.4 45.0 %copy-start.17 = (bf16[256,2048]{1,0:T(8,128)(2,1)S(1)}, bf16[256,2048]{1,0:T(8,128)(2,1)}, u32[]{:S(2)}) copy-start(bf16[256,2048]{1,0:T(8,128)(2,1)} %param.25) | copy-start | bytes 3145732
Sparse Core Ops, SparseCore 0:
  420.4 22.6 reduce-scatter.2
  445.6 23.7 reduce-scatter.4
where the time goes:
time: 479 us; the launch traced here: 478 us
  blocking collectives  252 us (53%)
  waiting for transfers between devices  95.4 us (20%)
  matrix products  48 us (10%)
  local copies, waits for them, and re-layouts  33.3 us (7%)
  other arithmetic  23.2 us (5%)
  between operations  14.4 us (3%)
  starting transfers between devices  11.9 us (2%)
    psum x1, blocking collectives, per_device(): summed = lax.psum(expert_term, 'mp')  191 us
    all_to_all x1, blocking collectives, per_device(): lax.all_to_all(outgoing, 'dp', split_axis=0, concat_axis=0, tiled=True)  61.4 us
    all_to_all x1, waiting for transfers between devices, per_device(): lax.all_to_all(result_rows, 'dp', split_axis=0, concat_axis=0, tiled=True)  41.5 us
    dot_general x1, matrix products, per_device(): jnp.dot(expert_inner, weight_out, preferred_element_type=jnp.float32)  27.6 us
    reduce_scatter x1, waiting for transfers between devices, per_device(): lax.psum_scatter(grad_term.astype(jnp.bfloat16), 'mp', scatter_dimension=...  24.2 us
    reduce_scatter x1, waiting for transfers between devices, per_device(): lax.psum_scatter(out_term.astype(jnp.bfloat16), 'mp', scatter_dimension=1...  18.7 us
    ppermute x2, waiting for transfers between devices, passed_along(): return lax.ppermute(value, axis, pairs)  11 us
  transfers between devices with their start and end apart: 5, of which 5 were waited for; matrix products, arithmetic and copies ran while one was open for 2% of the time, Pallas kernels for 0%

commit v1 on v0

--- a/solution.py
+++ b/solution.py
@@ -36,20 +36,21 @@
     return jnp.stack([leading, 1.0 - leading], 1)
 
 
-def slot_layout(route_rows, expert_count, capacity):
+def slot_tables(route_rows, expert_count, capacity):
     token_count = route_rows.shape[0]
-    flat_ids = route_rows.reshape(-1)
-    onehot = (flat_ids[:, None] == jnp.arange(expert_count, dtype=jnp.int32)[None, :]).astype(
-        jnp.int32
-    )
-    earlier = jnp.cumsum(onehot, 0) - onehot
-    slot_rank = jnp.sum(earlier * onehot, 1)
-    slot_index = flat_ids * capacity + slot_rank
-    pair_token = jnp.arange(2 * token_count, dtype=jnp.int32) // 2
-    slot_owner = (
-        jnp.full((expert_count * capacity,), token_count, jnp.int32).at[slot_index].set(pair_token)
-    )
-    return (slot_index, slot_owner)
+    expert_ids = jnp.arange(expert_count, dtype=jnp.int32)
+    hits = (route_rows[:, :, None] == expert_ids[None, None, :]).astype(jnp.bfloat16)
+    token_ids = jnp.arange(token_count)
+    below = (token_ids[:, None] > token_ids[None, :]).astype(jnp.bfloat16)
+    earlier = jnp.dot(below, hits.sum(1), preferred_element_type=jnp.float32)
+    rank = jnp.sum(earlier[:, None, :] * hits.astype(jnp.float32), -1).astype(jnp.int32)
+    slots = route_rows * capacity + rank
+    slot_ids = jnp.arange(expert_count * capacity, dtype=jnp.int32)
+    return slots[:, :, None] == slot_ids[None, None, :]
+
+
+def swapped(value):
+    return lax.ppermute(value, "mp", [(0, 1), (1, 0)])
 
 
 def contract_rows(left_rows, weight):
@@ -126,25 +127,46 @@
     normed = layer_norm(token_rows, norm_gain[0])
     route_rows = routes[0]
     gate_rows = gate_pairs(normed, router[0], route_rows)
-    slot_index, slot_owner = slot_layout(route_rows, expert_count, capacity)
+    places = slot_tables(route_rows, expert_count, capacity)
     weight_in = expert_in[0, 0]
     weight_out = expert_out[0, 0]
-    padded = jnp.concatenate([normed, jnp.zeros((1, normed.shape[1]), normed.dtype)], 0)
-    outgoing = padded[slot_owner].reshape(expert_count, capacity, normed.shape[1])
+    outgoing = lax.dot_general(
+        places.any(1).astype(jnp.bfloat16),
+        normed,
+        (((0,), (0,)), ((), ())),
+        preferred_element_type=jnp.float32,
+    ).astype(jnp.bfloat16)
+    outgoing = outgoing.reshape(expert_count, capacity, model_width)
     arrived = lax.all_to_all(outgoing, "dp", split_axis=0, concat_axis=0, tiled=True)
     slot_count = arrived.shape[1]
     expert_inner = jax.nn.relu(
         jnp.dot(arrived.reshape(-1, model_width), weight_in, preferred_element_type=jnp.float32)
     ).astype(jnp.bfloat16)
     expert_term = jnp.dot(expert_inner, weight_out, preferred_element_type=jnp.float32)
-    summed = lax.psum(expert_term, "mp")
-    result_rows = summed.astype(jnp.bfloat16).reshape(arrived.shape[0], slot_count, summed.shape[1])
+    result_rows = expert_term.astype(jnp.bfloat16).reshape(arrived.shape)
     returned_rows = lax.all_to_all(result_rows, "dp", split_axis=0, concat_axis=0, tiled=True)
-    picked_rows = returned_rows.reshape(expert_count * capacity, -1)[slot_index]
-    picked_rows = picked_rows.reshape(token_count, 2, -1).astype(jnp.float32)
-    mixed_rows = jnp.sum(gate_rows[:, :, None] * picked_rows, 1)
-    layer_state = (token_rows.astype(jnp.float32) + mixed_rows).astype(jnp.bfloat16)
-    state_half = lax.dynamic_slice_in_dim(layer_state, mp_index * half_width, half_width, 1)
+    returned_rows = returned_rows.reshape(expert_count * capacity, model_width)
+    mixing = jnp.sum(jnp.where(places, gate_rows[:, :, None], 0.0), 1)
+    coarse = mixing.astype(jnp.bfloat16)
+    fine = (mixing - coarse.astype(jnp.float32)).astype(jnp.bfloat16)
+    mixed_rows = jnp.dot(coarse, returned_rows, preferred_element_type=jnp.float32) + jnp.dot(
+        fine, returned_rows, preferred_element_type=jnp.float32
+    )
+
+    def own_half(value):
+        return lax.dynamic_slice_in_dim(value, mp_index * half_width, half_width, 1)
+
+    def other_half(value):
+        return lax.dynamic_slice_in_dim(value, (1 - mp_index) * half_width, half_width, 1)
+
+    mixed_half = own_half(mixed_rows) + swapped(other_half(mixed_rows).astype(jnp.bfloat16)).astype(jnp.float32)
+    state_half = (own_half(token_rows).astype(jnp.float32) + mixed_half).astype(jnp.bfloat16)
+    state_other = swapped(state_half)
+    layer_state = jnp.where(
+        mp_index == 0,
+        jnp.concatenate([state_half, state_other], 1),
+        jnp.concatenate([state_other, state_half], 1),
+    )
     proj_first = attn_weight[0, 0]
     proj_second = attn_weight[0, 1]
     projected = jnp.dot(layer_state, proj_first, preferred_element_type=jnp.float32).astype(
@@ -182,14 +204,8 @@
         return query_term
 
     grad_term = lax.cond(group_index == 0, encoder_grad, decoder_grad)
-    out_share, grad_share = (
-        lax.psum_scatter(
-            out_term.astype(jnp.bfloat16), "mp", scatter_dimension=1, tiled=True
-        ).astype(jnp.float32),
-        lax.psum_scatter(
-            grad_term.astype(jnp.bfloat16), "mp", scatter_dimension=1, tiled=True
-        ).astype(jnp.float32),
-    )
+    out_share = own_half(out_term) + swapped(other_half(out_term).astype(jnp.bfloat16)).astype(jnp.float32)
+    grad_share = own_half(grad_term) + swapped(other_half(grad_term).astype(jnp.bfloat16)).astype(jnp.float32)
     cot_half = lax.dynamic_slice_in_dim(cotangent, mp_index * half_width, half_width, 1)
     forward = jnp.where(
         group_index == 0,

time: 479 us -> 253 us (0.53)
  blocking collectives: 252 us -> 61.2 us
  local copies, waits for them, and re-layouts: 33.3 us -> 16 us
  between operations: 14.4 us -> 0.94 us
  other arithmetic: 23.2 us -> 13.7 us
  matrix products: 48 us -> 54.5 us
    psum x1 -> x0, blocking collectives: 191 us -> none  [per_device(): summed = lax.psum(expert_term, 'mp')]
    reduce_scatter x2 -> x0, waiting for transfers between devices: 42.9 us -> none  [the longest x1 24.2 us: per_device(): lax.psum_scatter(grad_term.astype(jnp.bfloat16), 'mp', scatter_dimension=...]
    ppermute x0 -> x4, waiting for transfers between devices: none -> 30.3 us  [swapped(): return lax.ppermute(value, 'mp', [(0, 1), (1, 0)])]
    gather x2 -> x0, local copies, waits for them, and re-layouts: 13.2 us -> none  [the longest x1 7.13 us: per_device(): picked_rows = returned_rows.reshape(expert_count * capacity, -1)[slot_index]]
    all_to_all x1, waiting for transfers between devices: 41.5 us -> 54 us  [per_device(): lax.all_to_all(result_rows, 'dp', split_axis=0, concat_axis=0, tiled=True)]
    reduce_sum x2, other arithmetic: 8.99 us -> 0.28 us  [the longest x1 0.27 us: per_device(): mixing = jnp.sum(jnp.where(places, gate_rows[:, :, None], 0.0), 1)]
    dot_general x0 -> x4, matrix products: none -> 8.52 us  [the longest x1 3.49 us: per_device(): jnp.dot(fine, returned_rows, preferred_element_type=jnp.float32)]
  transfers between devices with their start and end apart: 5 -> 7, of which waited for: 5 -> 6; matrix products, arithmetic and copies ran while one was open for 2% -> 4% of each run, Pallas kernels for 0% -> 0%
where the time goes in v1:
time: 253 us; the launch traced here: 249 us
  waiting for transfers between devices  90.7 us (36%)
  blocking collectives  61.2 us (24%)
  matrix products  54.5 us (22%)
  local copies, waits for them, and re-layouts  16 us (6%)
  other arithmetic  13.7 us (5%)
  starting transfers between devices  11.6 us (5%)
    all_to_all x1, blocking collectives, per_device(): lax.all_to_all(outgoing, 'dp', split_axis=0, concat_axis=0, tiled=True)  61.2 us
    all_to_all x1, waiting for transfers between devices, per_device(): lax.all_to_all(result_rows, 'dp', split_axis=0, concat_axis=0, tiled=True)  54 us
    ppermute x4, waiting for transfers between devices, swapped(): return lax.ppermute(value, 'mp', [(0, 1), (1, 0)])  30.3 us
    dot_general x1, matrix products, per_device(): jnp.dot(expert_inner, weight_out, preferred_element_type=jnp.float32)  25.4 us
    all_to_all x1, starting transfers between devices, per_device(): lax.all_to_all(result_rows, 'dp', split_axis=0, concat_axis=0, tiled=True)  6.91 us
    ppermute x2, waiting for transfers between devices, passed_along(): return lax.ppermute(value, axis, pairs)  6.35 us
    dot_general x2, matrix products, contract_rows(): lax.dot_general(left_rows, weight, (((1,), (1,)), ((), ())), preferred_el...  5.1 us
  transfers between devices with their start and end apart: 7, of which 6 were waited for; matrix products, arithmetic and copies ran while one was open for 4% of the time, Pallas kernels for 0%

profile of v1, /device:TPU:1, one launch (start us, length us, event | category | flops | bytes accessed | tf_op | source)
XLA Modules:
  0.0 248.5 jit_solution(14304626528771761330)
XLA Ops:
  0.7 1.5 convert_reduce_fusion
  2.2 1.6 fusion.32
  5.0 1.4 convolution_convert_fusion.4
  6.4 61.2 %all_to_all.10 = bf16[32,32,2048]{2,1,0:T(8,128)(2,1)} all-to-all(bf16[32,32,2048]{2,1,0:T(8,128)(2,1)S(1)} %bitcast.116), channel_id=1, replica_groups=mesh['grp'=2,'dp'=32,'mp'=2] {'dp'}, dimensions={0} | all-to-all | bytes 8388608 | tf_op jit(solution)/shard_map/all_to_all | solution.py:140
  67.6 25.4 %fusion.23 = bf16[1024,2048]{1,0:T(8,128)(2,1)} fusion(bf16[1,1,2048,2048]{3,2,1,0:T(8,128)(2,1)} %param.21, bf16[1024,2048]{1,0:T(8,128)(2,1)} %bitcast.118, bf16[1,1,2048,2048]{3,2,1,0:T(8,128)(2,1)} %param.20), kind=kOutput, calls=%fused_computation.33 | convolution fusion | flops 17186160640 | bytes 25165824 | tf_op jit(solution)/shard_map/dot_general | solution.py:145
  92.9 6.9 %all-to-all-start.1 = ((bf16[32,32,2048]{2,1,0:T(8,128)(2,1)}), bf16[32,32,2048]{2,1,0:T(8,128)(2,1)}, u32[]{:S(2)}, u32[]{:S(2)}) async-start(bf16[32,32,2048]{2,1,0:T(8,128)(2,1)} %bitcast.117), calls=%async_computation.1 | async-start | bytes 8388608 | tf_op jit(solution)/shard_map/all_to_all | solution.py:147
  100.2 54.0 %all-to-all-done.1 = bf16[32,32,2048]{2,1,0:T(8,128)(2,1)} async-done(((bf16[32,32,2048]{2,1,0:T(8,128)(2,1)}), bf16[32,32,2048]{2,1,0:T(8,128)(2,1)}, u32[]{:S(2)}, u32[]{:S(2)}) %all-to-all-start.1) | async-done | bytes 4194336 | tf_op jit(solution)/shard_map/all_to_all | solution.py:147
  154.2 3.4 %fusion.50 = f32[256,2048]{1,0:T(8,128)S(1)} fusion(bf16[1024,2048]{1,0:T(8,128)(2,1)} %bitcast.25, f32[256,1024]{1,0:T(8,128)S(1)} %select_reduce_fusion), kind=kOutput, calls=%fused_computation.76 | convolution fusion | flops 1074003968 | bytes 7340032 | tf_op jit(solution)/shard_map/dot_general | solution.py:152
  157.6 3.5 %convolution_add_fusion.1 = f32[256,2048]{1,0:T(8,128)S(1)} fusion(f32[256,2048]{1,0:T(8,128)S(1)} %fusion.50, bf16[1024,2048]{1,0:T(8,128)(2,1)} %bitcast.25, f32[256,1024]{1,0:T(8,128)S(1)} %select_reduce_fusion), kind=kOutput, calls=%fused_computation.38 | convolution fusion | flops 1075314688 | bytes 9437184 | tf_op jit(solution)/shard_map/dot_general | solution.py:152
  162.8 11.2 %collective-permute-done = bf16[256,1024]{1,0:T(8,128)(2,1)S(1)} collective-permute-done((bf16[256,1024]{1,0:T(8,128)(2,1)S(1)}, bf16[256,1024]{1,0:T(8,128)(2,1)S(1)}, u32[]{:S(2)}, u32[]{:S(2)}) %collective-permute-start) | collective-permute-done | bytes 524320 | tf_op jit(solution)/shard_map/ppermute | solution.py:53
  174.0 1.5 fusion.38
  175.7 4.0 %slice_bitcast_fusion.1 = (bf16[2048,512]{1,0:T(8,128)(2,1)}, bf16[2048,512]{1,0:T(8,128)(2,1)S(1)}) fusion(bf16[1,2,2048,512]{3,2,1,0:T(8,128)(2,1)} %param.22), kind=kLoop, calls=%fused_computation.49 | loop fusion | bytes 8388608 | tf_op jit(solution)/shard_map/squeeze | solution.py:170
  179.7 6.1 %collective-permute-done.1 = bf16[256,1024]{1,0:T(8,128)(2,1)S(1)} collective-permute-done((bf16[256,1024]{1,0:T(8,128)(2,1)S(1)}, bf16[256,1024]{1,0:T(8,128)(2,1)S(1)}, u32[]{:S(2)}, u32[]{:S(2)}) %collective-permute-start.1) | collective-permute-done | bytes 524320 | tf_op jit(solution)/shard_map/ppermute | solution.py:53
  189.3 6.3 %collective-permute-done.2 = bf16[2,256,512]{2,1,0:T(8,128)(2,1)} collective-permute-done((bf16[2,256,512]{2,1,0:T(8,128)(2,1)}, bf16[2,256,512]{2,1,0:T(8,128)(2,1)}, u32[]{:S(2)}, u32[]{:S(2)}) %collective-permute-start.2) | collective-permute-done | bytes 524320 | tf_op jit(solution)/shard_map/ppermute | solution.py:12
  195.6 26.9 %conditional.4 = (f32[256,2048]{1,0:T(8,128)}, bf16[2,256,512]{1,2,0:T(8,128)(2,1)}, f32[256,2048]{1,0:T(8,128)}) conditional(s32[]{:T(128)} %convert_element_type.163, () %tuple.34, (bf16[256,512]{1,0:T(8,128)(2,1)S(1)}, bf16[2,256,512]{2,1,0:T(8,128)(2,1)}, f32[256,256]{0,1:T(8,128)S(1)}, bf16[2048,512]{1,0:T(8,128)(2,1)S(1)}, ...), branch_computations={%region_9.10_spmd, %region_10.13_spmd} | conditional | flops 2085227264 | bytes 41164908 | solution.py:197
  195.6 1.9 convolution_convert_fusion.3
  198.5 2.0 copy.71
  202.4 2.3 fusion.59
  206.0 2.7 %convolution_convert_fusion.1 = bf16[4,256,128]{1,2,0:T(8,128)(2,1)} fusion(bf16[256,4,128]{0,2,1:T(8,128)(2,1)} %bitcast.130, f32[4,256,256]{1,2,0:T(8,128)} %fusion.2), kind=kOutput, calls=%fused_computation.9 | convolution fusion | flops 67765504 | bytes 1572864 | tf_op jit(solution)/shard_map/cond/branch_1_fun/hqk,khd->qhd/dot_general | solution.py:77
  208.7 2.7 %convolution_convert_fusion.2 = bf16[4,128,256]{2,1,0:T(8,128)(2,1)} fusion(bf16[256,4,128]{0,2,1:T(8,128)(2,1)} %bitcast.128, f32[4,256,256]{1,2,0:T(8,128)} %fusion.2), kind=kOutput, calls=%fused_computation.10 | convolution fusion | flops 67765504 | bytes 1572864 | tf_op jit(solution)/shard_map/cond/branch_1_fun/hqk,qhd->khd/dot_general | solution.py:98
  211.4 3.0 %fusion.58 = f32[256,2048]{1,0:T(8,128)} fusion(bf16[256,512]{0,1:T(8,128)(2,1)} %bitcast.132, bf16[2048,512]{1,0:T(8,128)(2,1)S(1)} %get-tuple-element.36), kind=kOutput, calls=%fused_computation.96 | convolution fusion | flops 536870912 | bytes 4456448 | tf_op jit(solution)/shard_map/cond/branch_1_fun/dot_general | solution.py:57
  214.4 2.8 %multiply_reduce_fusion = (f32[4,256]{1,0:T(4,128)S(1)}, f32[4,256,256]{1,2,0:T(8,128)}) fusion(f32[4,256,256]{1,2,0:T(8,128)} %fusion.59, bf16[256,4,128]{0,2,1:T(8,128)(2,1)S(1)} %bitcast.120, bf16[256,4,128]{0,2,1:T(8,128)(2,1)S(1)} %bitcast.123, f32[256,256]{0,1:T(8,128)S(1)} %get-tuple-element.35), kind=kOutput, calls=%fused_computation.13 | convolution fusion | flops 68419840 | bytes 2887680 | tf_op jit(solution)/shard_map/cond/branch_1_fun/div | solution.py:75
  217.1 1.7 multiply_convert_fusion
  220.5 2.1 fusion.60
  222.5 2.0 copy.72
  225.9 2.1 dynamic-slice_convert_fusion.1
  228.2 1.4 dynamic-slice_convert_fusion
  229.6 1.4 collective-permute-start.5
  231.0 5.3 %collective-permute-done.3 = bf16[256,1024]{1,0:T(8,128)(2,1)S(1)} collective-permute-done((bf16[256,1024]{1,0:T(8,128)(2,1)}, bf16[256,1024]{1,0:T(8,128)(2,1)S(1)}, u32[]{:S(2)}, u32[]{:S(2)}) %collective-permute-start.3) | collective-permute-done | bytes 524320 | tf_op jit(solution)/shard_map/ppermute | solution.py:53
  236.3 2.3 fusion.48
  238.5 7.8 %collective-permute-done.5 = bf16[256,1024]{1,0:T(8,128)(2,1)S(1)} collective-permute-done((bf16[256,1024]{1,0:T(8,128)(2,1)S(1)}, bf16[256,1024]{1,0:T(8,128)(2,1)S(1)}, u32[]{:S(2)}, u32[]{:S(2)}) %collective-permute-start.5) | collective-permute-done | bytes 524320 | tf_op jit(solution)/shard_map/ppermute | solution.py:53
  246.3 2.3 fusion.47
  (59 shorter events, 13.8 us)
Async XLA Ops:
  0.6 3.5 %copy-start = (bf16[1,2048,32]{1,2,0:T(8,128)(2,1)S(1)}, bf16[1,2048,32]{1,2,0:T(8,128)(2,1)}, u32[]{:S(2)}) copy-start(bf16[1,2048,32]{1,2,0:T(8,128)(2,1)} %param.18) | copy-start | bytes 393220
  0.6 3.4 %copy-start.3 = (bf16[1,256,2048]{2,1,0:T(8,128)(2,1)S(1)}, bf16[1,256,2048]{2,1,0:T(8,128)(2,1)}, u32[]{:S(2)}) copy-start(bf16[1,256,2048]{2,1,0:T(8,128)(2,1)} %param.16) | copy-start | bytes 3145732
  0.7 3.2 %copy-start.12 = (bf16[1,2048]{1,0:T(2,128)(2,1)S(1)}, bf16[1,2048]{1,0:T(2,128)(2,1)}, u32[]{:S(2)}) copy-start(bf16[1,2048]{1,0:T(2,128)(2,1)} %param.17) | copy-start | bytes 12292
  0.7 3.2 %copy-start.11 = (s32[1,256,2]{1,2,0:T(2,128)S(1)}, s32[1,256,2]{1,2,0:T(2,128)}, u32[]{:S(2)}) copy-start(s32[1,256,2]{1,2,0:T(2,128)} %param.19) | copy-start | bytes 6148
  92.9 61.2 %all-to-all-start.1 = ((bf16[32,32,2048]{2,1,0:T(8,128)(2,1)}), bf16[32,32,2048]{2,1,0:T(8,128)(2,1)}, u32[]{:S(2)}, u32[]{:S(2)}) async-start(bf16[32,32,2048]{2,1,0:T(8,128)(2,1)} %bitcast.117), calls=%async_computation.1 | async-start | bytes 8388608 | tf_op jit(solution)/shard_map/all_to_all | solution.py:147
  161.1 1.3 copy-start.5
  162.5 11.5 %collective-permute-start = (bf16[256,1024]{1,0:T(8,128)(2,1)S(1)}, bf16[256,1024]{1,0:T(8,128)(2,1)S(1)}, u32[]{:S(2)}, u32[]{:S(2)}) collective-permute-start(bf16[256,1024]{1,0:T(8,128)(2,1)S(1)} %dynamic-slice_convert_fusion.2), channel_id=1, source_target_pairs={{0,1},{1,0},{2,3},{3,2},{4,5},{5,4},{6,7},{7,6},{8,9},{9,8},{10,11... | collective-permute-start | bytes 1572872 | tf_op jit(solution)/shard_map/ppermute | solution.py:53
  175.5 10.4 %collective-permute-start.1 = (bf16[256,1024]{1,0:T(8,128)(2,1)S(1)}, bf16[256,1024]{1,0:T(8,128)(2,1)S(1)}, u32[]{:S(2)}, u32[]{:S(2)}) collective-permute-start(bf16[256,1024]{1,0:T(8,128)(2,1)S(1)} %fusion.38), channel_id=1, source_target_pairs={{0,1},{1,0},{2,3},{3,2},{4,5},{5,4},{6,7},{7,6},{8,9},{9,8},{10,11... | collective-permute-start | bytes 1572872 | tf_op jit(solution)/shard_map/ppermute | solution.py:53
  175.7 10.5 %copy-start.4 = (bf16[1,2,2048,512]{3,2,1,0:T(8,128)(2,1)S(1)}, bf16[1,2,2048,512]{3,2,1,0:T(8,128)(2,1)}, u32[]{:S(2)}) copy-start(bf16[1,2,2048,512]{3,2,1,0:T(8,128)(2,1)} %param.22) | copy-start | bytes 12582916
  187.0 2.2 copy-start.13
  187.0 2.2 copy-start.14
  187.9 7.8 %collective-permute-start.2 = (bf16[2,256,512]{2,1,0:T(8,128)(2,1)}, bf16[2,256,512]{2,1,0:T(8,128)(2,1)}, u32[]{:S(2)}, u32[]{:S(2)}) collective-permute-start(bf16[2,256,512]{2,1,0:T(8,128)(2,1)} %pad_maximum_fusion.1), channel_id=1, source_target_pairs={{0,64},{1,65},{2,66},{3,67},{4,68},{5,69},{6,70},{7,71},{8,72},{9,... | collective-permute-start | bytes 1572872 | tf_op jit(solution)/shard_map/ppermute | solution.py:12
  201.6 0.7 copy-start.6
  217.1 2.3 copy-start.10
  218.9 1.6 copy-start.2
  224.6 3.6 %collective-permute-start.4 = (bf16[2,256,512]{2,1,0:T(8,128)(2,1)}, bf16[2,256,512]{2,1,0:T(8,128)(2,1)S(1)}, u32[]{:S(2)}, u32[]{:S(2)}) collective-permute-start(bf16[2,256,512]{2,1,0:T(8,128)(2,1)} %copy.72), channel_id=1, source_target_pairs={{64,0},{65,1},{66,2},{67,3},{68,4},{69,5},{70,6},{71,7},{72,8},{73... | collective-permute-start | bytes 1572872 | tf_op jit(solution)/shard_map/ppermute | solution.py:12
  228.0 8.2 %collective-permute-start.3 = (bf16[256,1024]{1,0:T(8,128)(2,1)}, bf16[256,1024]{1,0:T(8,128)(2,1)S(1)}, u32[]{:S(2)}, u32[]{:S(2)}) collective-permute-start(bf16[256,1024]{1,0:T(8,128)(2,1)} %dynamic-slice_convert_fusion.1), channel_id=1, source_target_pairs={{0,1},{1,0},{2,3},{3,2},{4,5},{5,4},{6,7},{7,6},{8,9},{9,8},{10,11... | collective-permute-start | bytes 1572872 | tf_op jit(solution)/shard_map/ppermute | solution.py:53
  228.2 18.1 %copy-start.9 = (bf16[256,2048]{1,0:T(8,128)(2,1)S(1)}, bf16[256,2048]{1,0:T(8,128)(2,1)}, u32[]{:S(2)}) copy-start(bf16[256,2048]{1,0:T(8,128)(2,1)} %param.25) | copy-start | bytes 3145732
  228.2 20.3 %copy-start.1 = (bf16[1,2048,32]{1,2,0:T(8,128)(2,1)S(1)}, bf16[1,2048,32]{1,2,0:T(8,128)(2,1)}, u32[]{:S(2)}) copy-start(bf16[1,2048,32]{1,2,0:T(8,128)(2,1)} %param.18) | copy-start | bytes 393220
  229.6 16.7 %collective-permute-start.5 = (bf16[256,1024]{1,0:T(8,128)(2,1)S(1)}, bf16[256,1024]{1,0:T(8,128)(2,1)S(1)}, u32[]{:S(2)}, u32[]{:S(2)}) collective-permute-start(bf16[256,1024]{1,0:T(8,128)(2,1)S(1)} %dynamic-slice_convert_fusion), channel_id=1, source_target_pairs={{0,1},{1,0},{2,3},{3,2},{4,5},{5,4},{6,7},{7,6},{8,9},{9,8},{10,11... | collective-permute-start | bytes 1572872 | tf_op jit(solution)/shard_map/ppermute | solution.py:53

commit v2 on v1

--- a/solution.py
+++ b/solution.py
@@ -1,6 +1,8 @@
 import jax
 import jax.numpy as jnp
 from jax import lax
+from jax.experimental import pallas as pl
+from jax.experimental.pallas import tpu as pltpu
 from jax.sharding import PartitionSpec as P
 
 HEAD_DIM = 128
@@ -51,6 +53,252 @@
 
 def swapped(value):
     return lax.ppermute(value, "mp", [(0, 1), (1, 0)])
+
+
+RINGS = (2, 4, 4)
+SHARE = 512
+BOTH = 1024
+GROUP = 128
+BLOCK = 256
+TILE = 256
+
+
+def shortest(offset):
+    return sum(min(step, ring - step) for step, ring in zip(offset, RINGS))
+
+
+OFFSETS = sorted(
+    [(h, z, y) for h in range(RINGS[0]) for z in range(RINGS[1]) for y in range(RINGS[2])],
+    key=shortest,
+)
+
+
+def expert_kernel(
+    outgoing,
+    first_hbm,
+    second_hbm,
+    returned,
+    arrived,
+    inner,
+    first,
+    second,
+    for_partner,
+    from_partner,
+    both,
+    share,
+    load_sem,
+    own_sem,
+    send_sem,
+    recv_sem,
+    pass_sem,
+    passed_sem,
+    half_sem,
+    halved_sem,
+    back_sem,
+    came_sem,
+):
+    row, mp = lax.axis_index("dp"), lax.axis_index("mp")
+    cap = outgoing.shape[0] // len(OFFSETS)
+    width = outgoing.shape[1]
+    row_h, row_z, row_y = row // 16, row // 4 % 4, row % 4
+
+    def place(offset, sign):
+        dh, dz, dy = offset
+        index = (
+            (row_h + dh) % 2 * 16 + (row_z + sign * dz + 4) % 4 * 4 + (row_y + sign * dy + 4) % 4
+        )
+        return index, (mp + dh) % 2
+
+    def device(index, side):
+        return {"dp": index, "mp": side}
+
+    partner = device(row, 1 - mp)
+    barrier = pltpu.get_barrier_semaphore()
+    for offset in OFFSETS[1:]:
+        pl.semaphore_signal(barrier, inc=1, device_id=device(*place(offset, -1)), device_id_type=pl.DeviceIdType.MESH)
+    pl.semaphore_signal(barrier, inc=1, device_id=partner, device_id_type=pl.DeviceIdType.MESH)
+
+    loads = [
+        pltpu.make_async_copy(first_hbm, first, load_sem.at[0]),
+        pltpu.make_async_copy(second_hbm, second, load_sem.at[1]),
+    ]
+    for load in loads:
+        load.start()
+    pl.semaphore_wait(barrier, len(OFFSETS))
+
+    def remote(source, target, sent, landed, where):
+        return pltpu.make_async_remote_copy(
+            source, target, sent, landed, device_id=where, device_id_type=pl.DeviceIdType.MESH
+        )
+
+    def dispatch(slot, side, index, where):
+        columns = pl.ds(pl.multiple_of(side * SHARE, SHARE), SHARE + BOTH)
+        source = outgoing.at[pl.ds(pl.multiple_of(index * cap, cap), cap), columns]
+        target = arrived.at[pl.ds(slot * cap, cap), columns]
+        if slot == 0:
+            return pltpu.make_async_copy(source, target, own_sem.at[0])
+        return remote(source, target, send_sem.at[slot], recv_sem.at[slot], where)
+
+    sends = []
+    for slot, offset in enumerate(OFFSETS):
+        index, side = place(offset, 1)
+        sends.append(dispatch(slot, side, index, device(index, side)))
+        sends[slot].start()
+
+    def wait_arrival(slot):
+        if slot == 0:
+            sends[0].wait()
+        else:
+            dispatch(slot, mp, row, partner).wait_recv()
+
+    own_start = pl.multiple_of(mp * (SHARE + BOTH), SHARE)
+    their_start = pl.multiple_of((1 - mp) * (SHARE + BOTH), SHARE)
+
+    def forward(group, start):
+        region = arrived.at[pl.ds(group * GROUP, GROUP), pl.ds(start, SHARE)]
+        return remote(region, region, pass_sem.at[group], passed_sem.at[group], partner)
+
+    def up_project(block):
+        rows = pl.ds(block * BLOCK, BLOCK)
+
+        def step(tile, carry):
+            columns = pl.ds(pl.multiple_of(tile * TILE, TILE), TILE)
+            product = jnp.dot(arrived[rows, :], first[:, columns], preferred_element_type=jnp.float32)
+            inner[rows, columns] = jnp.maximum(product, 0.0).astype(jnp.bfloat16)
+            return carry
+
+        lax.fori_loop(0, inner.shape[1] // TILE, step, 0)
+
+    groups = arrived.shape[0] // GROUP
+    blocks = arrived.shape[0] // BLOCK
+    per_group = GROUP // cap
+    per_block = BLOCK // cap
+    forwards = [forward(group, own_start) for group in range(groups)]
+    for block in range(blocks + 1):
+        if block < blocks:
+            for group in range(block * BLOCK // GROUP, (block + 1) * BLOCK // GROUP):
+                for slot in range(group * per_group, (group + 1) * per_group):
+                    wait_arrival(slot)
+                forwards[group].start()
+        if block == 1:
+            loads[0].wait()
+        if block > 0:
+            for group in range((block - 1) * BLOCK // GROUP, block * BLOCK // GROUP):
+                forward(group, their_start).wait_recv()
+            up_project(block - 1)
+
+    def down_project(block, start, count, finish):
+        rows = pl.ds(block * BLOCK, BLOCK)
+
+        def step(tile, carry):
+            columns = pl.ds(pl.multiple_of(start + tile * TILE, TILE), TILE)
+            product = jnp.dot(inner[rows, :], second[:, columns], preferred_element_type=jnp.float32)
+            finish(rows, pl.ds(pl.multiple_of(tile * TILE, TILE), TILE), product)
+            return carry
+
+        lax.fori_loop(0, count // TILE, step, 0)
+
+    def keep_in(buffer):
+        def finish(rows, columns, product):
+            buffer[rows, columns] = product.astype(jnp.bfloat16)
+
+        return finish
+
+    def add_share(rows, columns, product):
+        total = product + from_partner[rows, columns].astype(jnp.float32)
+        share[rows, columns] = total.astype(jnp.bfloat16)
+
+    def halve(block):
+        rows = pl.ds(block * BLOCK, BLOCK)
+        return remote(for_partner.at[rows], from_partner.at[rows], half_sem.at[block], halved_sem.at[block], partner)
+
+    def give_back(slot, part, expert, where):
+        buffer, start, count = ((both, 0, BOTH), (share, BOTH, SHARE))[part]
+        source = buffer.at[pl.ds(slot * cap, cap)]
+        target = returned.at[pl.ds(pl.multiple_of(expert * cap, cap), cap), pl.ds(start, count)]
+        if slot == 0:
+            return pltpu.make_async_copy(source, target, own_sem.at[1 + part])
+        number = part * len(OFFSETS) + slot
+        return remote(source, target, back_sem.at[number], came_sem.at[number], where)
+
+    backs = []
+
+    def give_block_back(block, part):
+        for slot in range(block * per_block, (block + 1) * per_block):
+            back = give_back(slot, part, row, device(*place(OFFSETS[slot], -1)))
+            back.start()
+            backs.append((slot, back))
+
+    loads[1].wait()
+    halves = [halve(block) for block in range(blocks)]
+    for block in range(blocks):
+        down_project(block, their_start, SHARE, keep_in(for_partner))
+        halves[block].start()
+    for block in range(blocks):
+        down_project(block, SHARE, BOTH, keep_in(both))
+        give_block_back(block, 0)
+    for block in range(blocks):
+        halves[block].wait_recv()
+        down_project(block, own_start, SHARE, add_share)
+        give_block_back(block, 1)
+
+    for part in range(2):
+        for slot in range(1, len(OFFSETS)):
+            give_back(slot, part, place(OFFSETS[slot], 1)[0], partner).wait_recv()
+    for slot, back in backs:
+        if slot == 0:
+            back.wait()
+        else:
+            back.wait_send()
+    for slot in range(1, len(OFFSETS)):
+        sends[slot].wait_send()
+    for copy in forwards + halves:
+        copy.wait_send()
+
+
+def expert_exchange(outgoing, first, second):
+    slots, width = outgoing.shape
+    hidden = first.shape[1]
+    count = len(OFFSETS)
+    groups, blocks = slots // GROUP, slots // BLOCK
+    dma = pltpu.SemaphoreType.DMA
+    return pl.pallas_call(
+        expert_kernel,
+        out_shape=jax.ShapeDtypeStruct((slots, BOTH + SHARE), jnp.bfloat16),
+        in_specs=[
+            pl.BlockSpec(memory_space=pltpu.VMEM),
+            pl.BlockSpec(memory_space=pl.ANY),
+            pl.BlockSpec(memory_space=pl.ANY),
+        ],
+        out_specs=pl.BlockSpec(memory_space=pl.ANY),
+        scratch_shapes=[
+            pltpu.VMEM((slots, width), jnp.bfloat16),
+            pltpu.VMEM((slots, hidden), jnp.bfloat16),
+            pltpu.VMEM(first.shape, jnp.bfloat16),
+            pltpu.VMEM(second.shape, jnp.bfloat16),
+            pltpu.VMEM((slots, SHARE), jnp.bfloat16),
+            pltpu.VMEM((slots, SHARE), jnp.bfloat16),
+            pltpu.VMEM((slots, BOTH), jnp.bfloat16),
+            pltpu.VMEM((slots, SHARE), jnp.bfloat16),
+            dma((2,)),
+            dma((3,)),
+            dma((count,)),
+            dma((count,)),
+            dma((groups,)),
+            dma((groups,)),
+            dma((blocks,)),
+            dma((blocks,)),
+            dma((2 * count,)),
+            dma((2 * count,)),
+        ],
+        compiler_params=pltpu.CompilerParams(
+            collective_id=0, has_side_effects=True, vmem_limit_bytes=56 * 1024 * 1024
+        ),
+        cost_estimate=pl.CostEstimate(
+            flops=4 * slots * width * hidden, bytes_accessed=24 * 1024 * 1024, transcendentals=0
+        ),
+        name="expert_exchange",
+    )(outgoing, first, second)
 
 
 def contract_rows(left_rows, weight):
@@ -136,21 +384,30 @@
         (((0,), (0,)), ((), ())),
         preferred_element_type=jnp.float32,
     ).astype(jnp.bfloat16)
-    outgoing = outgoing.reshape(expert_count, capacity, model_width)
-    arrived = lax.all_to_all(outgoing, "dp", split_axis=0, concat_axis=0, tiled=True)
-    slot_count = arrived.shape[1]
-    expert_inner = jax.nn.relu(
-        jnp.dot(arrived.reshape(-1, model_width), weight_in, preferred_element_type=jnp.float32)
-    ).astype(jnp.bfloat16)
-    expert_term = jnp.dot(expert_inner, weight_out, preferred_element_type=jnp.float32)
-    result_rows = expert_term.astype(jnp.bfloat16).reshape(arrived.shape)
-    returned_rows = lax.all_to_all(result_rows, "dp", split_axis=0, concat_axis=0, tiled=True)
-    returned_rows = returned_rows.reshape(expert_count * capacity, model_width)
+    returned = expert_exchange(outgoing, weight_in, weight_out)
     mixing = jnp.sum(jnp.where(places, gate_rows[:, :, None], 0.0), 1)
     coarse = mixing.astype(jnp.bfloat16)
     fine = (mixing - coarse.astype(jnp.float32)).astype(jnp.bfloat16)
-    mixed_rows = jnp.dot(coarse, returned_rows, preferred_element_type=jnp.float32) + jnp.dot(
-        fine, returned_rows, preferred_element_type=jnp.float32
+
+    def mixed(weights, rows):
+        return jnp.dot(weights, rows, preferred_element_type=jnp.float32)
+
+    half_slots = expert_count * capacity // 2
+    my_side = lax.axis_index("dp") // (expert_count // 2)
+
+    def side_of(value, side, axis):
+        return lax.dynamic_slice_in_dim(value, side * half_slots, half_slots, axis)
+
+    def mixed_share(side):
+        rows = side_of(returned[:, BOTH:], side, 0)
+        return mixed(side_of(coarse, side, 1), rows) + mixed(side_of(fine, side, 1), rows)
+
+    mixed_both = mixed(coarse, returned[:, :BOTH]) + mixed(fine, returned[:, :BOTH])
+    mixed_own, mixed_other = mixed_share(my_side), mixed_share(1 - my_side)
+    mixed_rows = jnp.where(
+        mp_index == 0,
+        jnp.concatenate([mixed_own, mixed_both, mixed_other], 1),
+        jnp.concatenate([mixed_other, mixed_both, mixed_own], 1),
     )
 
     def own_half(value):

time: 253 us -> 217 us (0.86); the launches traced: 249 us -> 215 us
  Pallas kernels: 0 us -> 109 us
  blocking collectives: 61.2 us -> 0 us
  waiting for transfers between devices: 90.7 us -> 35.1 us
  matrix products: 54.5 us -> 33.1 us
  starting transfers between devices: 11.6 us -> 4.34 us
    pallas_call x0 -> x1, Pallas kernels: none -> 109 us  [expert_exchange(): pl.pallas_call(expert_kernel, out_shape=jax.ShapeDtypeStruct((slots, BOTH...]
    all_to_all x1 -> x0, blocking collectives: 61.2 us -> none  [per_device(): lax.all_to_all(outgoing, 'dp', split_axis=0, concat_axis=0, tiled=True)]
    all_to_all x1 -> x0, waiting for transfers between devices: 54 us -> none  [per_device(): lax.all_to_all(result_rows, 'dp', split_axis=0, concat_axis=0, tiled=True)]
    dot_general x3 -> x6, matrix products: 32.3 us -> 9.02 us  [mixed(): return jnp.dot(weights, rows, preferred_element_type=jnp.float32)]
    all_to_all x1 -> x0, starting transfers between devices: 6.91 us -> none  [per_device(): lax.all_to_all(result_rows, 'dp', split_axis=0, concat_axis=0, tiled=True)]
  transfers between devices with their start and end apart: 7 -> 6, of which waited for: 6 -> 5; matrix products, arithmetic and copies ran while one was open for 4% -> 5% of each run, Pallas kernels for 0% -> 0%
where the time goes in v2:
time: 217 us; the launch traced here: 215 us
  Pallas kernels  109 us (50%)
  waiting for transfers between devices  35.1 us (16%)
  matrix products  33.1 us (15%)
  local copies, waits for them, and re-layouts  17.1 us (8%)
  other arithmetic  16.2 us (7%)
  starting transfers between devices  4.34 us (2%)
    pallas_call x1, Pallas kernels, expert_exchange(): pl.pallas_call(expert_kernel, out_shape=jax.ShapeDtypeStruct((slots, BOTH...  109 us
    ppermute x4, waiting for transfers between devices, swapped(): return lax.ppermute(value, 'mp', [(0, 1), (1, 0)])  29.6 us
    dot_general x6, matrix products, mixed(): return jnp.dot(weights, rows, preferred_element_type=jnp.float32)  9.02 us
    ppermute x2, waiting for transfers between devices, passed_along(): return lax.ppermute(value, axis, pairs)  5.45 us
    dot_general x2, matrix products, contract_rows(): lax.dot_general(left_rows, weight, (((1,), (1,)), ((), ())), preferred_el...  5.09 us
    broadcast_in_dim x2, other arithmetic, per_device(): return (forward[None], backward[None])  4.51 us
  transfers between devices with their start and end apart: 6, of which 5 were waited for; matrix products, arithmetic and copies ran while one was open for 5% of the time, Pallas kernels for 0%

profile of v2, /device:TPU:1, one launch (start us, length us, event | category | flops | bytes accessed | tf_op | source)
XLA Modules:
  0.0 215.5 jit_solution(14629417162702441728)
XLA Ops:
  0.7 1.5 convert_reduce_fusion
  2.2 1.6 fusion.26
  5.4 3.4 %convolution_convert_fusion.4.outgoing = bf16[1024,2048]{1,0:T(8,128)(2,1)} fusion(pred[256,1024]{1,0:T(8,128)(4,1)S(1)} %fusion.29, bf16[1,256,2048]{2,1,0:T(8,128)(2,1)S(1)} %copy-done.3, f32[2048]{0:T(1024)S(1)} %bitcast.110, f32[256]{0:T(256)S(1)} %add_rsqrt_fusion, f32[256]{0:T(256)S(1)} %broadcast_multiply_fusion), kind=kOutput, calls=%fused_computation.28 | convolution fusion | flops 1078460416 | bytes 5515264 | tf_op jit(solution)/shard_map/dot_general | solution.py:381
  8.8 108.6 %expert_exchange.1 = bf16[1024,1536]{1,0:T(8,128)(2,1)} custom-call(bf16[1024,2048]{1,0:T(8,128)(2,1)} %convolution_convert_fusion.4.outgoing, bf16[2048,2048]{1,0:T(8,128)(2,1)} %bitcast.115, bf16[2048,2048]{1,0:T(8,128)(2,1)} %bitcast.116), custom_call_target="tpu_custom_call" | custom-call | flops 17179869184 | bytes 25165824 | tf_op jit(solution)/shard_map/expert_exchange/pallas_call | solution.py:265
  117.4 1.3 slice.34
  118.7 3.3 %fusion.30 = f32[256,1024]{1,0:T(8,128)} fusion(bf16[256,1024]{1,0:T(8,128)(2,1)S(1)} %get-tuple-element.76, bf16[1024,1536]{1,0:T(8,128)(2,1)} %expert_exchange.1), kind=kOutput, calls=%fused_computation.51 | convolution fusion | flops 536870912 | bytes 3670016 | tf_op jit(solution)/shard_map/dot_general | solution.py:393
  125.5 2.9 %fusion.34 = f32[256,1024]{1,0:T(8,128)} fusion(f32[256,1024]{1,0:T(8,128)} %fusion.30, bf16[256,1024]{1,0:T(8,128)(2,1)S(1)} %get-tuple-element.77, bf16[1024,1536]{1,0:T(8,128)(2,1)S(1)} %copy-done.7), kind=kOutput, calls=%fused_computation.55 | convolution fusion | flops 537133056 | bytes 4718592 | tf_op jit(solution)/shard_map/dot_general | solution.py:393
  128.4 2.1 fusion.18
  131.4 11.3 %collective-permute-done = bf16[256,1024]{1,0:T(8,128)(2,1)} collective-permute-done((bf16[256,1024]{1,0:T(8,128)(2,1)}, bf16[256,1024]{1,0:T(8,128)(2,1)}, u32[]{:S(2)}, u32[]{:S(2)}) %collective-permute-start) | collective-permute-done | bytes 524320 | tf_op jit(solution)/shard_map/ppermute | solution.py:55
  144.1 4.0 %slice_bitcast_fusion.1 = (bf16[2048,512]{1,0:T(8,128)(2,1)}, bf16[2048,512]{1,0:T(8,128)(2,1)S(1)}) fusion(bf16[1,2,2048,512]{3,2,1,0:T(8,128)(2,1)} %param.22), kind=kLoop, calls=%fused_computation.47 | loop fusion | bytes 8388608 | tf_op jit(solution)/shard_map/squeeze | solution.py:427
  148.1 6.1 %collective-permute-done.1 = bf16[256,1024]{1,0:T(8,128)(2,1)S(1)} collective-permute-done((bf16[256,1024]{1,0:T(8,128)(2,1)S(1)}, bf16[256,1024]{1,0:T(8,128)(2,1)S(1)}, u32[]{:S(2)}, u32[]{:S(2)}) %collective-permute-start.1) | collective-permute-done | bytes 524320 | tf_op jit(solution)/shard_map/ppermute | solution.py:55
  157.2 1.3 collective-permute-start.2
  159.3 5.4 %collective-permute-done.2 = bf16[2,256,512]{2,1,0:T(8,128)(2,1)S(1)} collective-permute-done((bf16[2,256,512]{2,1,0:T(8,128)(2,1)S(1)}, bf16[2,256,512]{2,1,0:T(8,128)(2,1)S(1)}, u32[]{:S(2)}, u32[]{:S(2)}) %collective-permute-start.2) | collective-permute-done | bytes 524320 | tf_op jit(solution)/shard_map/ppermute | solution.py:14
  164.7 24.8 %conditional.4 = (f32[256,2048]{1,0:T(8,128)}, bf16[2,256,512]{1,2,0:T(8,128)(2,1)}, f32[256,2048]{1,0:T(8,128)}) conditional(s32[]{:T(128)} %convert_element_type.155, () %tuple.34, (bf16[256,512]{1,0:T(8,128)(2,1)S(1)}, bf16[2,256,512]{2,1,0:T(8,128)(2,1)S(1)}, f32[256,256]{0,1:T(8,128)}, bf16[2048,512]{1,0:T(8,128)(2,1)S(1)}, ...), branch_computations={%region_9.10_spmd, %region_10.13_spmd} | conditional | flops 2085227264 | bytes 45359296 | solution.py:454
  164.7 2.1 convolution_convert_fusion.3
  169.8 1.3 fusion.71
  171.1 2.3 %fusion.2 = f32[4,256,256]{1,2,0:T(8,128)} fusion(bf16[256,4,128]{0,2,1:T(8,128)(2,1)S(1)} %bitcast.94, bf16[256,4,128]{0,2,1:T(8,128)(2,1)S(1)} %bitcast.97, f32[256,256]{0,1:T(8,128)} %get-tuple-element.35), kind=kOutput, calls=%fused_computation.4 | convolution fusion | flops 67633152 | bytes 1835008 | tf_op jit(solution)/shard_map/cond/branch_1_fun/qhd,khd->hqk/dot_general | solution.py:319
  173.4 2.7 %convolution_convert_fusion.1 = bf16[4,256,128]{1,2,0:T(8,128)(2,1)} fusion(bf16[256,4,128]{0,2,1:T(8,128)(2,1)} %bitcast.105, f32[4,256,256]{1,2,0:T(8,128)} %fusion.2), kind=kOutput, calls=%fused_computation.9 | convolution fusion | flops 67765504 | bytes 1572864 | tf_op jit(solution)/shard_map/cond/branch_1_fun/hqk,khd->qhd/dot_general | solution.py:325
  176.1 2.7 %convolution_convert_fusion.2 = bf16[4,128,256]{2,1,0:T(8,128)(2,1)} fusion(bf16[256,4,128]{0,2,1:T(8,128)(2,1)} %bitcast.103, f32[4,256,256]{1,2,0:T(8,128)} %fusion.2), kind=kOutput, calls=%fused_computation.10 | convolution fusion | flops 67765504 | bytes 1572864 | tf_op jit(solution)/shard_map/cond/branch_1_fun/hqk,qhd->khd/dot_general | solution.py:346
  178.8 3.0 %fusion.70 = f32[256,2048]{1,0:T(8,128)} fusion(bf16[256,512]{0,1:T(8,128)(2,1)} %bitcast.107, bf16[2048,512]{1,0:T(8,128)(2,1)S(1)} %get-tuple-element.36), kind=kOutput, calls=%fused_computation.112 | convolution fusion | flops 536870912 | bytes 4456448 | tf_op jit(solution)/shard_map/cond/branch_1_fun/dot_general | solution.py:305
  181.9 2.5 %multiply_reduce_fusion = (f32[4,256]{1,0:T(4,128)S(1)}, f32[4,256,256]{1,2,0:T(8,128)}) fusion(f32[4,256,256]{1,2,0:T(8,128)S(1)} %fusion.71, bf16[256,4,128]{0,2,1:T(8,128)(2,1)S(1)} %bitcast.95, bf16[256,4,128]{0,2,1:T(8,128)(2,1)} %bitcast.98, f32[256,256]{0,1:T(8,128)} %get-tuple-element.35), kind=kOutput, calls=%fused_computation.13 | convolution fusion | flops 68419840 | bytes 2887680 | tf_op jit(solution)/shard_map/cond/branch_1_fun/div | solution.py:323
  184.4 1.4 multiply_convert_fusion
  187.4 2.1 fusion.72
  189.5 2.1 copy.72
  191.6 1.3 collective-permute-start.4
  192.9 2.1 dynamic-slice_convert_fusion.1
  195.8 1.4 dynamic-slice_convert_fusion
  197.3 1.5 collective-permute-start.5
  198.8 4.5 %collective-permute-done.3 = bf16[256,1024]{1,0:T(8,128)(2,1)S(1)} collective-permute-done((bf16[256,1024]{1,0:T(8,128)(2,1)}, bf16[256,1024]{1,0:T(8,128)(2,1)S(1)}, u32[]{:S(2)}, u32[]{:S(2)}) %collective-permute-start.3) | collective-permute-done | bytes 524320 | tf_op jit(solution)/shard_map/ppermute | solution.py:55
  203.2 2.3 %fusion.49 = bf16[1,256,1024]{2,1,0:T(8,128)(2,1)} fusion(bf16[256,1024]{1,0:T(8,128)(2,1)S(1)} %copy-done.5, bf16[256,1024]{1,0:T(8,128)(2,1)S(1)} %collective-permute-done.3, f32[256,2048]{1,0:T(8,128)} %get-tuple-element.47, s32[]{:T(128)S(6)} %select_n.62, pred[]{:T(512)S(6)} %eq.28), kind=kLoop, calls=%fused_computation.78 | loop fusion | flops 1572864 | bytes 2621445 | tf_op jit(solution)/shard_map/broadcast_in_dim | solution.py:477
  205.5 7.7 %collective-permute-done.5 = bf16[256,1024]{1,0:T(8,128)(2,1)S(1)} collective-permute-done((bf16[256,1024]{1,0:T(8,128)(2,1)S(1)}, bf16[256,1024]{1,0:T(8,128)(2,1)S(1)}, u32[]{:S(2)}, u32[]{:S(2)}) %collective-permute-start.5) | collective-permute-done | bytes 524320 | tf_op jit(solution)/shard_map/ppermute | solution.py:55
  213.2 2.3 %fusion.48 = bf16[1,256,1024]{2,1,0:T(8,128)(2,1)} fusion(bf16[256,1024]{1,0:T(8,128)(2,1)S(1)} %collective-permute-done.5, f32[256,2048]{1,0:T(8,128)} %get-tuple-element.93, s32[]{:T(128)S(6)} %select_n.62, bf16[256,2048]{1,0:T(8,128)(2,1)S(1)} %copy-done.14, pred[]{:T(512)S(6)} %eq.28), kind=kLoop, calls=%fused_computation.77 | loop fusion | flops 1835008 | bytes 2621445 | tf_op jit(solution)/shard_map/broadcast_in_dim | solution.py:477
  (75 shorter events, 17.1 us)
Async XLA Ops:
  0.6 3.5 %copy-start = (bf16[1,2048,32]{1,2,0:T(8,128)(2,1)S(1)}, bf16[1,2048,32]{1,2,0:T(8,128)(2,1)}, u32[]{:S(2)}) copy-start(bf16[1,2048,32]{1,2,0:T(8,128)(2,1)} %param.18) | copy-start | bytes 393220
  0.6 3.5 %copy-start.3 = (bf16[1,256,2048]{2,1,0:T(8,128)(2,1)S(1)}, bf16[1,256,2048]{2,1,0:T(8,128)(2,1)}, u32[]{:S(2)}) copy-start(bf16[1,256,2048]{2,1,0:T(8,128)(2,1)} %param.16) | copy-start | bytes 3145732
  0.7 3.2 %copy-start.17 = (bf16[1,2048]{1,0:T(2,128)(2,1)S(1)}, bf16[1,2048]{1,0:T(2,128)(2,1)}, u32[]{:S(2)}) copy-start(bf16[1,2048]{1,0:T(2,128)(2,1)} %param.17) | copy-start | bytes 12292
  0.7 3.3 %copy-start.16 = (s32[1,256,2]{1,2,0:T(2,128)S(1)}, s32[1,256,2]{1,2,0:T(2,128)}, u32[]{:S(2)}) copy-start(s32[1,256,2]{1,2,0:T(2,128)} %param.19) | copy-start | bytes 6148
  123.4 2.1 copy-start.7
  131.3 11.4 %collective-permute-start = (bf16[256,1024]{1,0:T(8,128)(2,1)}, bf16[256,1024]{1,0:T(8,128)(2,1)}, u32[]{:S(2)}, u32[]{:S(2)}) collective-permute-start(bf16[256,1024]{1,0:T(8,128)(2,1)} %dynamic-slice_convert_fusion.2), channel_id=1, source_target_pairs={{0,1},{1,0},{2,3},{3,2},{4,5},{5,4},{6,7},{7,6},{8,9},{9,8},{10,11... | collective-permute-start | bytes 1572872 | tf_op jit(solution)/shard_map/ppermute | solution.py:55
  144.0 10.2 %copy-start.4 = (bf16[256,1024]{1,0:T(8,128)(2,1)}, bf16[256,1024]{1,0:T(8,128)(2,1)S(1)}, u32[]{:S(2)}) copy-start(bf16[256,1024]{1,0:T(8,128)(2,1)S(1)} %fusion.39) | copy-start | bytes 1572868
  144.0 10.2 %collective-permute-start.1 = (bf16[256,1024]{1,0:T(8,128)(2,1)S(1)}, bf16[256,1024]{1,0:T(8,128)(2,1)S(1)}, u32[]{:S(2)}, u32[]{:S(2)}) collective-permute-start(bf16[256,1024]{1,0:T(8,128)(2,1)S(1)} %fusion.39), channel_id=1, source_target_pairs={{0,1},{1,0},{2,3},{3,2},{4,5},{5,4},{6,7},{7,6},{8,9},{9,8},{10,11... | collective-permute-start | bytes 1572872 | tf_op jit(solution)/shard_map/ppermute | solution.py:55
  144.1 10.5 %copy-start.6 = (bf16[1,2,2048,512]{3,2,1,0:T(8,128)(2,1)S(1)}, bf16[1,2,2048,512]{3,2,1,0:T(8,128)(2,1)}, u32[]{:S(2)}) copy-start(bf16[1,2,2048,512]{3,2,1,0:T(8,128)(2,1)} %param.22) | copy-start | bytes 12582916
  155.4 3.1 %copy-start.18 = (s32[1,256]{1,0:T(1,128)S(1)}, s32[1,256]{1,0:T(1,128)}, u32[]{:S(2)}) copy-start(s32[1,256]{1,0:T(1,128)} %param.24) | copy-start | bytes 3076
  155.4 3.1 %copy-start.19 = (s32[1,256]{1,0:T(1,128)S(1)}, s32[1,256]{1,0:T(1,128)}, u32[]{:S(2)}) copy-start(s32[1,256]{1,0:T(1,128)} %param.23) | copy-start | bytes 3076
  157.2 7.6 %collective-permute-start.2 = (bf16[2,256,512]{2,1,0:T(8,128)(2,1)S(1)}, bf16[2,256,512]{2,1,0:T(8,128)(2,1)S(1)}, u32[]{:S(2)}, u32[]{:S(2)}) collective-permute-start(bf16[2,256,512]{2,1,0:T(8,128)(2,1)S(1)} %pad_maximum_fusion.3), channel_id=1, source_target_pairs={{0,64},{1,65},{2,66},{3,67},{4,68},{5,69},{6,70},{7,71},{8,72},{9,... | collective-permute-start | bytes 1572872 | tf_op jit(solution)/shard_map/ppermute | solution.py:14
  164.7 3.0 %copy-start.13 = (bf16[2,256,512]{2,1,0:T(8,128)(2,1)}, bf16[2,256,512]{2,1,0:T(8,128)(2,1)S(1)}, u32[]{:S(2)}) copy-start(bf16[2,256,512]{2,1,0:T(8,128)(2,1)S(1)} %get-tuple-element.69) | copy-start | bytes 1572868 | tf_op jit(solution)/shard_map/cond
  169.1 0.7 copy-start.10
  169.1 2.0 copy-start.8
  184.4 1.4 copy-start.9
  184.4 2.0 copy-start.15
  185.8 1.6 copy-start.2
  191.6 3.4 %collective-permute-start.4 = (bf16[2,256,512]{2,1,0:T(8,128)(2,1)}, bf16[2,256,512]{2,1,0:T(8,128)(2,1)S(1)}, u32[]{:S(2)}, u32[]{:S(2)}) collective-permute-start(bf16[2,256,512]{2,1,0:T(8,128)(2,1)} %copy.72), channel_id=1, source_target_pairs={{64,0},{65,1},{66,2},{67,3},{68,4},{69,5},{70,6},{71,7},{72,8},{73... | collective-permute-start | bytes 1572872 | tf_op jit(solution)/shard_map/ppermute | solution.py:14
  195.0 8.2 %collective-permute-start.3 = (bf16[256,1024]{1,0:T(8,128)(2,1)}, bf16[256,1024]{1,0:T(8,128)(2,1)S(1)}, u32[]{:S(2)}, u32[]{:S(2)}) collective-permute-start(bf16[256,1024]{1,0:T(8,128)(2,1)} %dynamic-slice_convert_fusion.1), channel_id=1, source_target_pairs={{0,1},{1,0},{2,3},{3,2},{4,5},{5,4},{6,7},{7,6},{8,9},{9,8},{10,11... | collective-permute-start | bytes 1572872 | tf_op jit(solution)/shard_map/ppermute | solution.py:55
  195.0 0.8 copy-start.11
  195.8 7.4 %copy-start.5 = (bf16[256,1024]{1,0:T(8,128)(2,1)S(1)}, bf16[256,1024]{1,0:T(8,128)(2,1)}, u32[]{:S(2)}) copy-start(bf16[256,1024]{1,0:T(8,128)(2,1)} %copy-done.4) | copy-start | bytes 1572868
  195.8 17.4 %copy-start.14 = (bf16[256,2048]{1,0:T(8,128)(2,1)S(1)}, bf16[256,2048]{1,0:T(8,128)(2,1)}, u32[]{:S(2)}) copy-start(bf16[256,2048]{1,0:T(8,128)(2,1)} %param.25) | copy-start | bytes 3145732
  195.8 19.7 %copy-start.1 = (bf16[1,2048,32]{1,2,0:T(8,128)(2,1)S(1)}, bf16[1,2048,32]{1,2,0:T(8,128)(2,1)}, u32[]{:S(2)}) copy-start(bf16[1,2048,32]{1,2,0:T(8,128)(2,1)} %param.18) | copy-start | bytes 393220
  197.3 16.0 %collective-permute-start.5 = (bf16[256,1024]{1,0:T(8,128)(2,1)S(1)}, bf16[256,1024]{1,0:T(8,128)(2,1)S(1)}, u32[]{:S(2)}, u32[]{:S(2)}) collective-permute-start(bf16[256,1024]{1,0:T(8,128)(2,1)S(1)} %dynamic-slice_convert_fusion), channel_id=1, source_target_pairs={{0,1},{1,0},{2,3},{3,2},{4,5},{5,4},{6,7},{7,6},{8,9},{9,8},{10,11... | collective-permute-start | bytes 1572872 | tf_op jit(solution)/shard_map/ppermute | solution.py:55

commit v3 on v2

--- a/solution.py
+++ b/solution.py
@@ -6,12 +6,6 @@
 from jax.sharding import PartitionSpec as P
 
 HEAD_DIM = 128
-
-
-def passed_along(value, axis, by):
-    peers = lax.axis_size(axis)
-    pairs = [(i, i + by) for i in range(peers) if 0 <= i + by < peers]
-    return lax.ppermute(value, axis, pairs)
 
 
 def layer_norm(token_rows, gain_row):
@@ -49,10 +43,6 @@
     slots = route_rows * capacity + rank
     slot_ids = jnp.arange(expert_count * capacity, dtype=jnp.int32)
     return slots[:, :, None] == slot_ids[None, None, :]
-
-
-def swapped(value):
-    return lax.ppermute(value, "mp", [(0, 1), (1, 0)])
 
 
 RINGS = (2, 4, 4)
@@ -307,50 +297,268 @@
     )
 
 
-def cross_attend(query_rows, key_rows, value_rows, seg_mask, cot_rows, query_weight, out_weight):
-    token_count = query_rows.shape[0]
-    source_count = key_rows.shape[0]
-    head_count = query_rows.shape[1] // HEAD_DIM
+def sum_rows(left, right):
+    return lax.dot_general(left, right, (((0,), (0,)), ((), ())), preferred_element_type=jnp.float32)
+
+
+def attend_head(query, key, value, grad, matches):
     softmax_scale = HEAD_DIM ** (-0.5)
-    query_heads = query_rows.reshape(token_count, head_count, HEAD_DIM)
-    key_heads = key_rows.reshape(source_count, head_count, HEAD_DIM)
-    value_heads = value_rows.reshape(source_count, head_count, HEAD_DIM)
-    scores = (
-        jnp.einsum("qhd,khd->hqk", query_heads, key_heads, preferred_element_type=jnp.float32)
-        * softmax_scale
-    )
-    exp_scores = jnp.exp(scores) * seg_mask[None]
+    scores = contract_rows(query, key) * softmax_scale
+    exp_scores = jnp.where(matches, jnp.exp(scores), 0.0)
     weights = exp_scores / jnp.sum(exp_scores, -1, keepdims=True)
     weights_b = weights.astype(jnp.bfloat16)
-    context = jnp.einsum(
-        "hqk,khd->qhd", weights_b, value_heads, preferred_element_type=jnp.float32
-    ).astype(jnp.bfloat16)
-    out_term = contract_rows(context.reshape(token_count, -1), out_weight)
-    context_grad = jnp.dot(cot_rows, out_weight, preferred_element_type=jnp.float32).astype(
-        jnp.bfloat16
-    )
-    grad_heads = context_grad.reshape(token_count, head_count, HEAD_DIM)
-    prob_grad = jnp.einsum(
-        "qhd,khd->hqk", grad_heads, value_heads, preferred_element_type=jnp.float32
-    )
+    context = jnp.dot(weights_b, value, preferred_element_type=jnp.float32)
+    prob_grad = contract_rows(grad, value)
     row_delta = jnp.sum(weights * prob_grad, -1, keepdims=True)
     score_grad = (weights * (prob_grad - row_delta)).astype(jnp.bfloat16)
-    query_grad = (
-        jnp.einsum("hqk,khd->qhd", score_grad, key_heads, preferred_element_type=jnp.float32)
-        * softmax_scale
-    ).astype(jnp.bfloat16)
-    key_grad = (
-        jnp.einsum("hqk,qhd->khd", score_grad, query_heads, preferred_element_type=jnp.float32)
-        * softmax_scale
-    ).astype(jnp.bfloat16)
-    value_grad = jnp.einsum(
-        "hqk,qhd->khd", weights_b, grad_heads, preferred_element_type=jnp.float32
-    ).astype(jnp.bfloat16)
-    query_term = contract_rows(query_grad.reshape(token_count, -1), query_weight)
-    key_value_grads = jnp.stack(
-        [key_grad.reshape(source_count, -1), value_grad.reshape(source_count, -1)]
-    )
-    return (out_term, query_term, key_value_grads)
+    query_grad = jnp.dot(score_grad, key, preferred_element_type=jnp.float32) * softmax_scale
+    key_grad = sum_rows(score_grad, query) * softmax_scale
+    value_grad = sum_rows(weights_b, grad)
+    return [part.astype(jnp.bfloat16) for part in (key_grad, value_grad, query_grad, context)]
+
+
+def layer_kernel(
+    returned,
+    coarse,
+    fine,
+    hidden,
+    cotangent,
+    weight_hbm,
+    src_row,
+    tgt_column,
+    forward,
+    backward,
+    weight,
+    mix_out,
+    mix_in,
+    own_mix,
+    state,
+    projected,
+    held,
+    grads,
+    final_out,
+    final_in,
+    load_sem,
+    mix_sent,
+    mix_here,
+    state_sent,
+    state_here,
+    held_sent,
+    held_here,
+    grad_sent,
+    grad_here,
+    final_sent,
+    final_here,
+):
+    group, row, mp = lax.axis_index("grp"), lax.axis_index("dp"), lax.axis_index("mp")
+    partner, core = {"mp": 1 - mp}, {"grp": 1 - group}
+    barrier = pltpu.get_barrier_semaphore()
+    for where in (partner, core):
+        pl.semaphore_signal(barrier, inc=1, device_id=where, device_id_type=pl.DeviceIdType.MESH)
+    load = pltpu.make_async_copy(weight_hbm, weight, load_sem.at[0])
+    load.start()
+
+    def remote(source, target, sent, landed, where):
+        return pltpu.make_async_remote_copy(
+            source, target, sent, landed, device_id=where, device_id_type=pl.DeviceIdType.MESH
+        )
+
+    half = BOTH
+    my_side = row // 16
+    slots = returned.shape[0]
+
+    def span(start, count=SHARE):
+        return pl.ds(pl.multiple_of(start, SHARE), count)
+
+    def mix_rows(rows, columns):
+        values = returned[rows, columns]
+        return jnp.dot(coarse[:, rows], values, preferred_element_type=jnp.float32) + jnp.dot(
+            fine[:, rows], values, preferred_element_type=jnp.float32
+        )
+
+    def mix_part(part, side):
+        if part == 0:
+            return mix_rows(pl.ds(0, slots), span(side * SHARE))
+        which = (my_side + (side - mp) * (side - mp)) % 2
+        return mix_rows(span(which * (slots // 2), slots // 2), pl.ds(BOTH, SHARE))
+
+    def piece(part, side):
+        return span(SHARE + side * SHARE) if part == 0 else span(side * (SHARE + BOTH))
+
+    mixes = [
+        remote(mix_out.at[part], mix_in.at[part], mix_sent.at[part], mix_here.at[part], partner)
+        for part in range(2)
+    ]
+    pl.semaphore_wait(barrier, 2)
+    for part in range(2):
+        mix_out[part] = mix_part(part, 1 - mp).astype(jnp.bfloat16)
+        mixes[part].start()
+    for part in range(2):
+        own_mix[part] = mix_part(part, mp)
+
+    def project(source, which, columns):
+        return jnp.dot(source[:, columns], weight[which, columns, :], preferred_element_type=jnp.float32)
+
+    load.wait()
+
+    @pl.when(group == 1)
+    def _():
+        projected[1] = project(cotangent, 1, pl.ds(0, 2 * half))
+
+    def hand_state(part, side):
+        region = state.at[:, piece(part, side)]
+        return remote(region, region, state_sent.at[part], state_here.at[part], partner)
+
+    hands = [hand_state(part, mp) for part in range(2)]
+    for part in range(2):
+        mixes[part].wait_recv()
+        columns = piece(part, mp)
+        total = hidden[:, columns].astype(jnp.float32) + (
+            own_mix[part] + mix_in[part].astype(jnp.float32)
+        )
+        state[:, columns] = total.astype(jnp.bfloat16)
+        hands[part].start()
+
+    order = [(0, mp), (1, mp), (0, 1 - mp), (1, 1 - mp)]
+    for number, (part, side) in enumerate(order):
+        if number >= 2:
+            hand_state(part, side).wait_recv()
+        columns = piece(part, side)
+        term = project(state, 0, columns)
+        projected[0] = term if number == 0 else projected[0] + term
+
+        @pl.when(group == 0)
+        def _():
+            other = project(state, 1, columns)
+            projected[1] = other if number == 0 else projected[1] + other
+
+    pair = 2 * HEAD_DIM
+    for which in range(2):
+        for heads in range(2):
+            held[group, which, heads] = projected[which, :, heads * pair : (heads + 1) * pair].astype(
+                jnp.bfloat16
+            )
+
+    def hand_held(which, owner, heads):
+        region = held.at[owner, which, heads]
+        return remote(region, region, held_sent.at[which], held_here.at[which], core)
+
+    handed = [hand_held(which, group, 1 - group) for which in range(2)]
+    for which in range(2):
+        handed[which].start()
+    matches = tgt_column[...] == src_row[...]
+    for which in range(2):
+        hand_held(which, 1 - group, group).wait_recv()
+
+    for head in range(2):
+        columns = slice(head * HEAD_DIM, (head + 1) * HEAD_DIM)
+        results = attend_head(
+            held[1, 0, group][:, columns],
+            held[0, 0, group][:, columns],
+            held[0, 1, group][:, columns],
+            held[1, 1, group][:, columns],
+            matches,
+        )
+        for number, result in enumerate(results):
+            grads[number // 2, number % 2, group, :, columns] = result
+
+    def hand_grad(which, owner, heads):
+        region = grads.at[owner, which, heads]
+        return remote(region, region, grad_sent.at[which], grad_here.at[which], core)
+
+    given = [hand_grad(which, 1 - group, group) for which in range(2)]
+    for which in range(2):
+        given[which].start()
+    for which in range(2):
+        hand_grad(which, group, 1 - group).wait_recv()
+
+    def back_project(which, start):
+        rows = span(start)
+        return contract_rows(grads[group, which, 0], weight[which, rows, :pair]) + contract_rows(
+            grads[group, which, 1], weight[which, rows, pair:]
+        )
+
+    def final(which, chunk):
+        number = which * 2 + chunk
+        return remote(
+            final_out.at[number], final_in.at[number], final_sent.at[number], final_here.at[number], partner
+        )
+
+    @pl.when(group == 0)
+    def _():
+        for chunk in range(2):
+            start = (1 - mp) * half + chunk * SHARE
+            final_out[chunk] = (back_project(0, start) + back_project(1, start)).astype(jnp.bfloat16)
+            final(0, chunk).start()
+        forward[...] = state[:, span(mp * half, half)]
+        for chunk in range(2):
+            start = mp * half + chunk * SHARE
+            own = back_project(0, start) + back_project(1, start)
+            final(0, chunk).wait_recv()
+            backward[:, chunk * SHARE : (chunk + 1) * SHARE] = (
+                own + final_in[chunk].astype(jnp.float32)
+            ).astype(jnp.bfloat16)
+        for chunk in range(2):
+            final(0, chunk).wait_send()
+
+    @pl.when(group == 1)
+    def _():
+        for which in range(2):
+            for chunk in range(2):
+                start = (1 - mp) * half + chunk * SHARE
+                final_out[which * 2 + chunk] = back_project(which, start).astype(jnp.bfloat16)
+                final(which, chunk).start()
+        for which, base, target in ((0, cotangent, backward), (1, state, forward)):
+            for chunk in range(2):
+                start = mp * half + chunk * SHARE
+                own = back_project(which, start)
+                final(which, chunk).wait_recv()
+                total = base[:, span(start)].astype(jnp.float32) + (
+                    own + final_in[which * 2 + chunk].astype(jnp.float32)
+                )
+                target[:, chunk * SHARE : (chunk + 1) * SHARE] = total.astype(jnp.bfloat16)
+        for which in range(2):
+            for chunk in range(2):
+                final(which, chunk).wait_send()
+
+    for copy in mixes + hands + handed + given:
+        copy.wait_send()
+
+
+def finish_layer(returned, coarse, fine, hidden, cotangent, weight, src_row, tgt_column):
+    tokens, width = hidden.shape
+    half = width // 2
+    dma = pltpu.SemaphoreType.DMA
+    vmem = pl.BlockSpec(memory_space=pltpu.VMEM)
+    pair = 2 * HEAD_DIM
+    return pl.pallas_call(
+        layer_kernel,
+        out_shape=[jax.ShapeDtypeStruct((tokens, half), jnp.bfloat16)] * 2,
+        in_specs=[vmem] * 5 + [pl.BlockSpec(memory_space=pl.ANY)] + [vmem] * 2,
+        out_specs=[vmem] * 2,
+        scratch_shapes=[
+            pltpu.VMEM(weight.shape, jnp.bfloat16),
+            pltpu.VMEM((2, tokens, SHARE), jnp.bfloat16),
+            pltpu.VMEM((2, tokens, SHARE), jnp.bfloat16),
+            pltpu.VMEM((2, tokens, SHARE), jnp.float32),
+            pltpu.VMEM((tokens, width), jnp.bfloat16),
+            pltpu.VMEM((2, tokens, 2 * pair), jnp.float32),
+            pltpu.VMEM((2, 2, 2, tokens, pair), jnp.bfloat16),
+            pltpu.VMEM((2, 2, 2, tokens, pair), jnp.bfloat16),
+            pltpu.VMEM((4, tokens, SHARE), jnp.bfloat16),
+            pltpu.VMEM((4, tokens, SHARE), jnp.bfloat16),
+            dma((1,)),
+        ]
+        + [dma((2,))] * 8
+        + [dma((4,))] * 2,
+        compiler_params=pltpu.CompilerParams(
+            collective_id=1, has_side_effects=True, vmem_limit_bytes=48 * 1024 * 1024
+        ),
+        cost_estimate=pl.CostEstimate(
+            flops=12 * tokens * width * half, bytes_accessed=12 * 1024 * 1024, transcendentals=131072
+        ),
+        name="finish_layer",
+    )(returned, coarse, fine, hidden, cotangent, weight, src_row, tgt_column)
 
 
 def per_device(
@@ -365,13 +573,10 @@
     tgt_segments,
     cotangent,
 ):
-    group_index = lax.axis_index("grp")
-    mp_index = lax.axis_index("mp")
     expert_count = lax.axis_size("dp")
     token_rows = hidden_in[0]
     token_count, model_width = token_rows.shape
     capacity = 4 * token_count // expert_count
-    half_width = model_width // lax.axis_size("mp")
     normed = layer_norm(token_rows, norm_gain[0])
     route_rows = routes[0]
     gate_rows = gate_pairs(normed, router[0], route_rows)
@@ -388,91 +593,15 @@
     mixing = jnp.sum(jnp.where(places, gate_rows[:, :, None], 0.0), 1)
     coarse = mixing.astype(jnp.bfloat16)
     fine = (mixing - coarse.astype(jnp.float32)).astype(jnp.bfloat16)
-
-    def mixed(weights, rows):
-        return jnp.dot(weights, rows, preferred_element_type=jnp.float32)
-
-    half_slots = expert_count * capacity // 2
-    my_side = lax.axis_index("dp") // (expert_count // 2)
-
-    def side_of(value, side, axis):
-        return lax.dynamic_slice_in_dim(value, side * half_slots, half_slots, axis)
-
-    def mixed_share(side):
-        rows = side_of(returned[:, BOTH:], side, 0)
-        return mixed(side_of(coarse, side, 1), rows) + mixed(side_of(fine, side, 1), rows)
-
-    mixed_both = mixed(coarse, returned[:, :BOTH]) + mixed(fine, returned[:, :BOTH])
-    mixed_own, mixed_other = mixed_share(my_side), mixed_share(1 - my_side)
-    mixed_rows = jnp.where(
-        mp_index == 0,
-        jnp.concatenate([mixed_own, mixed_both, mixed_other], 1),
-        jnp.concatenate([mixed_other, mixed_both, mixed_own], 1),
-    )
-
-    def own_half(value):
-        return lax.dynamic_slice_in_dim(value, mp_index * half_width, half_width, 1)
-
-    def other_half(value):
-        return lax.dynamic_slice_in_dim(value, (1 - mp_index) * half_width, half_width, 1)
-
-    mixed_half = own_half(mixed_rows) + swapped(other_half(mixed_rows).astype(jnp.bfloat16)).astype(jnp.float32)
-    state_half = (own_half(token_rows).astype(jnp.float32) + mixed_half).astype(jnp.bfloat16)
-    state_other = swapped(state_half)
-    layer_state = jnp.where(
-        mp_index == 0,
-        jnp.concatenate([state_half, state_other], 1),
-        jnp.concatenate([state_other, state_half], 1),
-    )
-    proj_first = attn_weight[0, 0]
-    proj_second = attn_weight[0, 1]
-    projected = jnp.dot(layer_state, proj_first, preferred_element_type=jnp.float32).astype(
-        jnp.bfloat16
-    )
-
-    def encoder_values():
-        return jnp.dot(layer_state, proj_second, preferred_element_type=jnp.float32).astype(
-            jnp.bfloat16
-        )
-
-    def absent_values():
-        return jnp.zeros_like(projected)
-
-    value_rows = lax.cond(group_index == 0, encoder_values, absent_values)
-    handed = passed_along(jnp.stack([projected, value_rows]), "grp", 1)
-    seg_mask = (tgt_segments[0][:, None] == src_segments[0][None, :]).astype(jnp.float32)
-
-    def decoder_side():
-        return cross_attend(
-            projected, handed[0], handed[1], seg_mask, cotangent, proj_first, proj_second
-        )
-
-    def encoder_side():
-        zero_rows = jnp.zeros((token_count, model_width), jnp.float32)
-        return (zero_rows, zero_rows, jnp.zeros_like(handed))
-
-    out_term, query_term, key_value_grads = lax.cond(group_index == 1, decoder_side, encoder_side)
-    grads_in = passed_along(key_value_grads, "grp", -1)
-
-    def encoder_grad():
-        return contract_rows(grads_in[0], proj_first) + contract_rows(grads_in[1], proj_second)
-
-    def decoder_grad():
-        return query_term
-
-    grad_term = lax.cond(group_index == 0, encoder_grad, decoder_grad)
-    out_share = own_half(out_term) + swapped(other_half(out_term).astype(jnp.bfloat16)).astype(jnp.float32)
-    grad_share = own_half(grad_term) + swapped(other_half(grad_term).astype(jnp.bfloat16)).astype(jnp.float32)
-    cot_half = lax.dynamic_slice_in_dim(cotangent, mp_index * half_width, half_width, 1)
-    forward = jnp.where(
-        group_index == 0,
-        state_half,
-        (state_half.astype(jnp.float32) + out_share).astype(jnp.bfloat16),
-    )
-    backward = jnp.where(
-        group_index == 0,
-        grad_share.astype(jnp.bfloat16),
-        (cot_half.astype(jnp.float32) + grad_share).astype(jnp.bfloat16),
+    forward, backward = finish_layer(
+        returned,
+        coarse,
+        fine,
+        token_rows,
+        cotangent,
+        attn_weight[0],
+        src_segments,
+        tgt_segments.reshape(token_count, 1),
     )
     return (forward[None], backward[None])
 

time: 217 us -> 173 us (0.80)
  Pallas kernels: 109 us -> 161 us
  waiting for transfers between devices: 35.1 us -> 0 us
  matrix products: 33.1 us -> 4.03 us
  local copies, waits for them, and re-layouts: 17.1 us -> 2.37 us
  other arithmetic: 16.2 us -> 4.68 us
  starting transfers between devices: 4.34 us -> 0 us
    pallas_call x0 -> x1, Pallas kernels: none -> 52.4 us  [finish_layer(): pl.pallas_call(layer_kernel, out_shape=[jax.ShapeDtypeStruct((tokens, hal...]
    ppermute x6 -> x0, waiting for transfers between devices: 35.1 us -> none  [the longest x4 29.6 us: swapped(): return lax.ppermute(value, 'mp', [(0, 1), (1, 0)])]
    dot_general x16 -> x0, matrix products: 26.5 us -> none  [the longest x6 9.02 us: mixed(): return jnp.dot(weights, rows, preferred_element_type=jnp.float32)]
    broadcast_in_dim x2 -> x0, other arithmetic: 4.51 us -> none  [per_device(): return (forward[None], backward[None])]
    convert_element_type x3 -> x0, local copies, waits for them, and re-layouts: 4.4 us -> none  [the longest x1 2.1 us: per_device(): other_half(out_term).astype(jnp.bfloat16)]
    ppermute x6 -> x0, starting transfers between devices: 4.34 us -> none  [the longest x2 2.6 us: passed_along(): return lax.ppermute(value, axis, pairs)]
    squeeze x1 -> x0, local copies, waits for them, and re-layouts: 4 us -> none  [per_device(): proj_first = attn_weight[0, 0]]
    convert_element_type x3 -> x0, other arithmetic: 3.5 us -> none  [the longest x1 1.43 us: cross_attend(): score_grad = (weights * (prob_grad - row_delta)).astype(jnp.bfloat16)]
  transfers between devices with their start and end apart: 6 -> 0, of which waited for: 5 -> 0; matrix products, arithmetic and copies ran while one was open for 5% -> 0% of each run, Pallas kernels for 0% -> 0%
where the time goes in v3:
time: 173 us
  Pallas kernels  161 us (93%)
  other arithmetic  4.68 us (3%)
  matrix products  4.03 us (2%)
  local copies, waits for them, and re-layouts  2.37 us (1%)
    pallas_call x1, Pallas kernels, expert_exchange(): pl.pallas_call(expert_kernel, out_shape=jax.ShapeDtypeStruct((slots, BOTH...  109 us
    pallas_call x1, Pallas kernels, finish_layer(): pl.pallas_call(layer_kernel, out_shape=[jax.ShapeDtypeStruct((tokens, hal...  52.4 us

profile of v3, /device:TPU:1, one launch (start us, length us, event | category | flops | bytes accessed | tf_op | source)
XLA Modules:
  0.0 172.9 jit_solution(3224386351680802501)
XLA Ops:
  0.6 0.0 copy-start
  0.6 0.0 copy-start.1
  0.7 0.8 mul.67
  1.5 0.0 copy-start.4
  1.5 1.4 convert_reduce_fusion
  2.9 1.6 fusion.2
  4.6 0.0 copy-done
  4.6 0.0 copy-done.1
  4.6 0.5 fusion.11
  5.1 0.0 copy-done.4
  5.1 0.2 fusion.13
  5.3 0.1 select_reduce_fusion.1
  5.4 0.3 fusion.5
  5.6 3.4 %convolution_convert_fusion.outgoing = bf16[1024,2048]{1,0:T(8,128)(2,1)} fusion(pred[256,1024]{1,0:T(8,128)(4,1)S(1)} %fusion.5, f32[2048]{0:T(1024)S(1)} %bitcast.28, f32[256]{0:T(256)S(1)} %add_rsqrt_fusion, f32[256]{0:T(256)S(1)} %broadcast_multiply_fusion, bf16[1,256,2048]{2,1,0:T(8,128)(2,1)S(1)} %copy-done.1), kind=kOutput, calls=%fused_computation | convolution fusion | flops 1078460416 | bytes 5515264 | tf_op jit(solution)/shard_map/dot_general | solution.py:586
  9.0 108.7 %expert_exchange.1.returned = bf16[1024,1536]{1,0:T(8,128)(2,1)} custom-call(bf16[1024,2048]{1,0:T(8,128)(2,1)} %convolution_convert_fusion.outgoing, bf16[2048,2048]{1,0:T(8,128)(2,1)} %bitcast.32, bf16[2048,2048]{1,0:T(8,128)(2,1)} %bitcast.33), custom_call_target="tpu_custom_call" | custom-call | flops 17179869184 | bytes 25165824 | tf_op jit(solution)/shard_map/expert_exchange/pallas_call | solution.py:255
  117.7 0.0 copy-start.5
  117.7 0.0 copy-start.2
  117.7 0.0 copy-start.3
  117.7 0.3 select_reduce_fusion
  118.0 0.1 subtract_convert_fusion
  118.2 0.2 copy-done.5
  118.4 0.1 copy.27.tgt_column
  118.5 0.4 copy-done.2
  118.9 0.0 copy-done.3
  118.9 52.4 %finish_layer.1 = (bf16[256,1024]{1,0:T(8,128)(2,1)S(1)}, bf16[256,1024]{1,0:T(8,128)(2,1)S(1)}) custom-call(bf16[1024,1536]{1,0:T(8,128)(2,1)} %expert_exchange.1.returned, bf16[256,1024]{1,0:T(8,128)(2,1)S(1)} %get-tuple-element.9.coarse, bf16[256,1024]{1,0:T(8,128)(2,1)S(1)} %get-tuple-element.8.fine, bf16[256,2048]{1,0:T(8,128)(2,1)S(1)} %bitcast.24, ...), custom_call_target="tpu_custom_call" | custom-call | flops 6442450944 | bytes 12582912 | tf_op jit(solution)/shard_map/finish_layer/pallas_call | solution.py:534
  171.3 0.8 copy.30
  172.1 0.8 copy.31
  (6 shorter events, 0.1 us)
Async XLA Ops:
  0.6 4.0 %copy-start = (bf16[1,2048,32]{1,2,0:T(8,128)(2,1)S(1)}, bf16[1,2048,32]{1,2,0:T(8,128)(2,1)}, u32[]{:S(2)}) copy-start(bf16[1,2048,32]{1,2,0:T(8,128)(2,1)} %param.12) | copy-start | bytes 393220
  0.6 4.0 %copy-start.1 = (bf16[1,256,2048]{2,1,0:T(8,128)(2,1)S(1)}, bf16[1,256,2048]{2,1,0:T(8,128)(2,1)}, u32[]{:S(2)}) copy-start(bf16[1,256,2048]{2,1,0:T(8,128)(2,1)} %param.10) | copy-start | bytes 3145732
  1.5 3.7 %copy-start.4 = (s32[1,256,2]{1,2,0:T(2,128)S(1)}, s32[1,256,2]{1,2,0:T(2,128)}, u32[]{:S(2)}) copy-start(s32[1,256,2]{1,2,0:T(2,128)} %param.13) | copy-start | bytes 6148
  117.7 0.7 copy-start.5
  117.7 1.2 copy-start.2
  117.7 1.2 copy-start.3

commit v4 on v3

v4 whole, which is shorter than its diff:
```python
import jax
import jax.numpy as jnp
from jax import lax
from jax.experimental import pallas as pl
from jax.experimental.pallas import tpu as pltpu
from jax.sharding import PartitionSpec as P

HEAD_DIM = 128


RINGS = (2, 4, 4)
SHARE = 512
BOTH = 1024
GROUP = 128
BLOCK = 256
TILE = 256


def shortest(offset):
    return sum(min(step, ring - step) for step, ring in zip(offset, RINGS))


OFFSETS = sorted(
    [(h, z, y) for h in range(RINGS[0]) for z in range(RINGS[1]) for y in range(RINGS[2])],
    key=shortest,
)


def contract_rows(left_rows, weight):
    return lax.dot_general(
        left_rows, weight, (((1,), (1,)), ((), ())), preferred_element_type=jnp.float32
    )


def sum_rows(left, right):
    return lax.dot_general(left, right, (((0,), (0,)), ((), ())), preferred_element_type=jnp.float32)


def attend_head(query, key, value, grad, matches):
    softmax_scale = HEAD_DIM ** (-0.5)
    scores = contract_rows(query, key) * softmax_scale
    exp_scores = jnp.where(matches, jnp.exp(scores), 0.0)
    weights = exp_scores / jnp.sum(exp_scores, -1, keepdims=True)
    weights_b = weights.astype(jnp.bfloat16)
    context = jnp.dot(weights_b, value, preferred_element_type=jnp.float32)
    prob_grad = contract_rows(grad, value)
    row_delta = jnp.sum(weights * prob_grad, -1, keepdims=True)
    score_grad = (weights * (prob_grad - row_delta)).astype(jnp.bfloat16)
    query_grad = jnp.dot(score_grad, key, preferred_element_type=jnp.float32) * softmax_scale
    key_grad = sum_rows(score_grad, query) * softmax_scale
    value_grad = sum_rows(weights_b, grad)
    return [part.astype(jnp.bfloat16) for part in (key_grad, value_grad, query_grad, context)]


def layer_kernel(
    hidden,
    gain,
    router,
    routes,
    routes_t,
    src_row,
    tgt_column,
    first_hbm,
    second_hbm,
    weight_hbm,
    cotangent_hbm,
    forward,
    backward,
    normed,
    outgoing,
    arrived,
    inner,
    first,
    second,
    weight,
    cotangent,
    coarse,
    fine,
    for_partner,
    from_partner,
    both,
    share,
    returned,
    mix_out,
    mix_in,
    own_mix,
    state,
    projected,
    held,
    grads,
    final_out,
    final_in,
    load_sem,
    own_sem,
    send_sem,
    recv_sem,
    pass_sem,
    passed_sem,
    half_sem,
    halved_sem,
    back_sem,
    came_sem,
    mix_sent,
    mix_here,
    state_sent,
    state_here,
    held_sent,
    held_here,
    grad_sent,
    grad_here,
    final_sent,
    final_here,
):
    group, row, mp = lax.axis_index("grp"), lax.axis_index("dp"), lax.axis_index("mp")
    experts = len(OFFSETS)
    slots, width = outgoing.shape
    tokens = hidden.shape[0]
    cap = slots // experts
    half = width // 2
    row_h, row_z, row_y = row // 16, row // 4 % 4, row % 4
    partner, core = {"mp": 1 - mp}, {"grp": 1 - group}

    def place(offset, sign):
        dh, dz, dy = offset
        index = (
            (row_h + dh) % 2 * 16 + (row_z + sign * dz + 4) % 4 * 4 + (row_y + sign * dy + 4) % 4
        )
        return index, (mp + dh) % 2

    def device(index, side):
        return {"dp": index, "mp": side}

    def remote(source, target, sent, landed, where):
        return pltpu.make_async_remote_copy(
            source, target, sent, landed, device_id=where, device_id_type=pl.DeviceIdType.MESH
        )

    def span(start, count=SHARE):
        return pl.ds(pl.multiple_of(start, SHARE), count)

    barrier = pltpu.get_barrier_semaphore()
    greeted = [device(*place(offset, -1)) for offset in OFFSETS[1:]] + [partner, core]
    for where in greeted:
        pl.semaphore_signal(barrier, inc=1, device_id=where, device_id_type=pl.DeviceIdType.MESH)
    loads = [
        pltpu.make_async_copy(source, target, load_sem.at[number])
        for number, (source, target) in enumerate(
            ((first_hbm, first), (weight_hbm, weight), (cotangent_hbm, cotangent), (second_hbm, second))
        )
    ]
    for load in loads:
        load.start()

    norm_rows = 64

    def normalise(step, carry):
        rows = pl.ds(pl.multiple_of(step * norm_rows, norm_rows), norm_rows)
        values = hidden[rows, :].astype(jnp.float32)
        centred = values - jnp.mean(values, -1, keepdims=True)
        variance = jnp.mean(centred * centred, -1, keepdims=True)
        scaled = centred * lax.rsqrt(variance + 1e-05) * gain[...].astype(jnp.float32)
        normed[rows, :] = scaled.astype(jnp.bfloat16)
        return carry

    lax.fori_loop(0, tokens // norm_rows, normalise, 0)

    def iota(shape, axis):
        return lax.broadcasted_iota(jnp.int32, shape, axis)

    def ones_where(mask):
        return jnp.where(mask, 1.0, 0.0)

    square = (tokens, tokens)
    named_t = [routes_t[k : k + 1, :] == iota((experts, tokens), 0) for k in range(2)]
    earlier_t = jnp.dot(
        (ones_where(named_t[0]) + ones_where(named_t[1])).astype(jnp.bfloat16),
        ones_where(iota(square, 0) < iota(square, 1)).astype(jnp.bfloat16),
        preferred_element_type=jnp.float32,
    )
    rank_t = [jnp.sum(jnp.where(mask, earlier_t, 0.0), 0, keepdims=True) for mask in named_t]
    places = iota((cap, tokens), 0).astype(jnp.float32)

    def slot_rows(slot):
        expert = place(OFFSETS[slot], 1)[0]
        rank = jnp.where(
            routes_t[0:1, :] == expert, rank_t[0], jnp.where(routes_t[1:2, :] == expert, rank_t[1], -1.0)
        )
        return ones_where(rank == places)

    def dispatch(slot, part, side, where):
        columns = span(side * (SHARE + BOTH)) if part == 0 else pl.ds(SHARE, BOTH)
        source = outgoing.at[pl.ds(slot * cap, cap), columns]
        target = arrived.at[pl.ds(slot * cap, cap), columns]
        if slot == 0:
            return pltpu.make_async_copy(source, target, own_sem.at[part])
        number = part * experts + slot
        return remote(source, target, send_sem.at[number], recv_sem.at[number], where)

    sends = []

    def send(slot, part):
        index, side = place(OFFSETS[slot], 1)
        sends.append((slot, part, dispatch(slot, part, side, device(index, side))))
        sends[-1][2].start()

    blocks = slots // BLOCK
    per_block = BLOCK // cap
    for block in range(blocks):
        chosen = jnp.concatenate(
            [slot_rows(slot) for slot in range(block * per_block, (block + 1) * per_block)], 0
        ).astype(jnp.bfloat16)
        for start in range(0, width, SHARE):
            outgoing[block * BLOCK : (block + 1) * BLOCK, start : start + SHARE] = jnp.dot(
                chosen, normed[:, start : start + SHARE], preferred_element_type=jnp.float32
            ).astype(jnp.bfloat16)
        if block == 0:
            pl.semaphore_wait(barrier, len(greeted))
        for slot in range(block * per_block, (block + 1) * per_block):
            send(slot, 0)
    for slot in range(experts):
        send(slot, 1)

    named = [routes[:, k : k + 1] == iota((tokens, experts), 1) for k in range(2)]
    earlier = jnp.dot(
        ones_where(iota(square, 0) > iota(square, 1)).astype(jnp.bfloat16),
        (ones_where(named[0]) + ones_where(named[1])).astype(jnp.bfloat16),
        preferred_element_type=jnp.float32,
    )
    logits = jnp.dot(normed[...], router[...], preferred_element_type=jnp.float32)

    def chosen_of(values, k):
        return jnp.sum(jnp.where(named[k], values, 0.0), 1, keepdims=True)

    leading = jax.nn.sigmoid(chosen_of(logits, 0) - chosen_of(logits, 1))
    gates = (leading, 1.0 - leading)
    spots = [routes[:, k : k + 1] * cap + chosen_of(earlier, k).astype(jnp.int32) for k in range(2)]
    for start in range(0, slots, BLOCK):
        columns = iota((tokens, BLOCK), 1) + start
        mixing = jnp.where(spots[0] == columns, gates[0], 0.0) + jnp.where(spots[1] == columns, gates[1], 0.0)
        rough = mixing.astype(jnp.bfloat16)
        coarse[:, start : start + BLOCK] = rough
        fine[:, start : start + BLOCK] = (mixing - rough.astype(jnp.float32)).astype(jnp.bfloat16)

    def wait_arrival(slot, part):
        if slot == 0:
            sends[0 if part == 0 else experts][2].wait()
        else:
            dispatch(slot, part, mp, partner).wait_recv()

    own_start = mp * (SHARE + BOTH)
    their_start = (1 - mp) * (SHARE + BOTH)

    def pass_on(number, start):
        region = arrived.at[pl.ds(number * GROUP, GROUP), span(start)]
        return remote(region, region, pass_sem.at[number], passed_sem.at[number], partner)

    groups = slots // GROUP
    per_group = GROUP // cap
    passes = [pass_on(number, own_start) for number in range(groups)]
    for number in range(groups):
        for slot in range(number * per_group, (number + 1) * per_group):
            wait_arrival(slot, 0)
        passes[number].start()

    def project(source, which, columns):
        return jnp.dot(source[:, columns], weight[which, columns, :], preferred_element_type=jnp.float32)

    for load in loads[:3]:
        load.wait()

    @pl.when(group == 1)
    def _():
        projected[1] = project(cotangent, 1, pl.ds(0, width))

    def up_project(block):
        rows = pl.ds(block * BLOCK, BLOCK)

        def step(tile, carry):
            columns = pl.ds(pl.multiple_of(tile * TILE, TILE), TILE)
            product = jnp.dot(arrived[rows, :], first[:, columns], preferred_element_type=jnp.float32)
            inner[rows, columns] = jnp.maximum(product, 0.0).astype(jnp.bfloat16)
            return carry

        lax.fori_loop(0, inner.shape[1] // TILE, step, 0)

    for block in range(blocks):
        for number in range(block * BLOCK // GROUP, (block + 1) * BLOCK // GROUP):
            pass_on(number, their_start).wait_recv()
        for slot in range(block * per_block, (block + 1) * per_block):
            wait_arrival(slot, 1)
        up_project(block)

    def down_project(block, start, count, finish):
        rows = pl.ds(block * BLOCK, BLOCK)

        def step(tile, carry):
            columns = pl.ds(pl.multiple_of(start + tile * TILE, TILE), TILE)
            product = jnp.dot(inner[rows, :], second[:, columns], preferred_element_type=jnp.float32)
            finish(rows, pl.ds(pl.multiple_of(tile * TILE, TILE), TILE), product)
            return carry

        lax.fori_loop(0, count // TILE, step, 0)

    def keep_in(buffer):
        def finish(rows, columns, product):
            buffer[rows, columns] = product.astype(jnp.bfloat16)

        return finish

    def add_share(rows, columns, product):
        total = product + from_partner[rows, columns].astype(jnp.float32)
        share[rows, columns] = total.astype(jnp.bfloat16)

    def halve(block):
        rows = pl.ds(block * BLOCK, BLOCK)
        return remote(for_partner.at[rows], from_partner.at[rows], half_sem.at[block], halved_sem.at[block], partner)

    def give_back(slot, part, expert, where):
        buffer, start, count = ((both, 0, BOTH), (share, BOTH, SHARE))[part]
        source = buffer.at[pl.ds(slot * cap, cap)]
        target = returned.at[pl.ds(pl.multiple_of(expert * cap, cap), cap), pl.ds(start, count)]
        if slot == 0:
            return pltpu.make_async_copy(source, target, own_sem.at[2 + part])
        number = part * experts + slot
        return remote(source, target, back_sem.at[number], came_sem.at[number], where)

    backs = []

    def give_block_back(block, part):
        for slot in range(block * per_block, (block + 1) * per_block):
            backs.append((slot, part, give_back(slot, part, row, device(*place(OFFSETS[slot], -1)))))
            backs[-1][2].start()

    loads[3].wait()
    halves = [halve(block) for block in range(blocks)]
    for block in range(blocks):
        down_project(block, their_start, SHARE, keep_in(for_partner))
        halves[block].start()
    for block in range(blocks):
        down_project(block, SHARE, BOTH, keep_in(both))
        give_block_back(block, 0)
    for block in range(blocks):
        halves[block].wait_recv()
        down_project(block, own_start, SHARE, add_share)
        give_block_back(block, 1)

    def mix_rows(rows, columns):
        values = returned[rows, columns]
        return jnp.dot(coarse[:, rows], values, preferred_element_type=jnp.float32) + jnp.dot(
            fine[:, rows], values, preferred_element_type=jnp.float32
        )

    def mix_part(part, mine):
        if part == 0:
            return mix_rows(pl.ds(0, slots), span((mp if mine else 1 - mp) * SHARE))
        which = row_h if mine else 1 - row_h
        return mix_rows(span(which * (slots // 2), slots // 2), pl.ds(BOTH, SHARE))

    def piece(part, side):
        return span(SHARE + side * SHARE) if part == 0 else span(side * (SHARE + BOTH))

    mixes = [
        remote(mix_out.at[part], mix_in.at[part], mix_sent.at[part], mix_here.at[part], partner)
        for part in range(2)
    ]

    def hand_state(part, side):
        region = state.at[:, piece(part, side)]
        return remote(region, region, state_sent.at[part], state_here.at[part], partner)

    hands = [hand_state(part, mp) for part in range(2)]

    def project_piece(part, side, opening):
        columns = piece(part, side)
        term = project(state, 0, columns)
        projected[0] = term if opening else projected[0] + term

        @pl.when(group == 0)
        def _():
            other = project(state, 1, columns)
            projected[1] = other if opening else projected[1] + other

    for part in range(2):
        for slot in range(experts):
            if slot > 0:
                give_back(slot, part, place(OFFSETS[slot], 1)[0], partner).wait_recv()
            else:
                backs[part * experts][2].wait()
        mix_out[part] = mix_part(part, False).astype(jnp.bfloat16)
        mixes[part].start()
        own_mix[part] = mix_part(part, True)
        mixes[part].wait_recv()
        columns = piece(part, mp)
        total = hidden[:, columns].astype(jnp.float32) + (
            own_mix[part] + mix_in[part].astype(jnp.float32)
        )
        state[:, columns] = total.astype(jnp.bfloat16)
        hands[part].start()
        project_piece(part, mp, part == 0)
    for part in range(2):
        hand_state(part, 1 - mp).wait_recv()
        project_piece(part, 1 - mp, False)

    pair = 2 * HEAD_DIM
    for which in range(2):
        for heads in range(2):
            held[group, which, heads] = projected[which, :, heads * pair : (heads + 1) * pair].astype(
                jnp.bfloat16
            )

    def hand_held(which, owner, heads):
        region = held.at[owner, which, heads]
        return remote(region, region, held_sent.at[which], held_here.at[which], core)

    handed = [hand_held(which, group, 1 - group) for which in range(2)]
    for which in range(2):
        handed[which].start()
    matches = tgt_column[...] == src_row[...]
    for which in range(2):
        hand_held(which, 1 - group, group).wait_recv()

    for head in range(2):
        columns = slice(head * HEAD_DIM, (head + 1) * HEAD_DIM)
        results = attend_head(
            held[1, 0, group][:, columns],
            held[0, 0, group][:, columns],
            held[0, 1, group][:, columns],
            held[1, 1, group][:, columns],
            matches,
        )
        for number, result in enumerate(results):
            grads[number // 2, number % 2, group, :, columns] = result

    def hand_grad(which, owner, heads):
        region = grads.at[owner, which, heads]
        return remote(region, region, grad_sent.at[which], grad_here.at[which], core)

    given = [hand_grad(which, 1 - group, group) for which in range(2)]
    for which in range(2):
        given[which].start()
    for which in range(2):
        hand_grad(which, group, 1 - group).wait_recv()

    def back_project(which, start):
        rows = span(start)
        return contract_rows(grads[group, which, 0], weight[which, rows, :pair]) + contract_rows(
            grads[group, which, 1], weight[which, rows, pair:]
        )

    def final(which, chunk):
        number = which * 2 + chunk
        return remote(
            final_out.at[number], final_in.at[number], final_sent.at[number], final_here.at[number], partner
        )

    @pl.when(group == 0)
    def _():
        for chunk in range(2):
            start = (1 - mp) * half + chunk * SHARE
            final_out[chunk] = (back_project(0, start) + back_project(1, start)).astype(jnp.bfloat16)
            final(0, chunk).start()
        forward[...] = state[:, span(mp * half, half)]
        for chunk in range(2):
            start = mp * half + chunk * SHARE
            own = back_project(0, start) + back_project(1, start)
            final(0, chunk).wait_recv()
            backward[:, chunk * SHARE : (chunk + 1) * SHARE] = (
                own + final_in[chunk].astype(jnp.float32)
            ).astype(jnp.bfloat16)
        for chunk in range(2):
            final(0, chunk).wait_send()

    @pl.when(group == 1)
    def _():
        for which in range(2):
            for chunk in range(2):
                start = (1 - mp) * half + chunk * SHARE
                final_out[which * 2 + chunk] = back_project(which, start).astype(jnp.bfloat16)
                final(which, chunk).start()
        for which, base, target in ((0, cotangent, backward), (1, state, forward)):
            for chunk in range(2):
                start = mp * half + chunk * SHARE
                own = back_project(which, start)
                final(which, chunk).wait_recv()
                total = base[:, span(start)].astype(jnp.float32) + (
                    own + final_in[which * 2 + chunk].astype(jnp.float32)
                )
                target[:, chunk * SHARE : (chunk + 1) * SHARE] = total.astype(jnp.bfloat16)
        for which in range(2):
            for chunk in range(2):
                final(which, chunk).wait_send()

    for slot, part, copy in sends + backs:
        if slot > 0:
            copy.wait_send()
    for copy in passes + halves + mixes + hands + handed + given:
        copy.wait_send()


def whole_layer(hidden, gain, router, routes, src_row, tgt_column, first, second, weight, cotangent):
    tokens, width = hidden.shape
    half, inner = width // 2, first.shape[1]
    experts = router.shape[1]
    slots = 4 * tokens
    pair = 2 * HEAD_DIM
    dma = pltpu.SemaphoreType.DMA
    vmem = pl.BlockSpec(memory_space=pltpu.VMEM)
    shapes = [
        (tokens, width),
        (slots, width),
        (slots, width),
        (slots, inner),
        first.shape,
        second.shape,
        weight.shape,
        cotangent.shape,
        (tokens, slots),
        (tokens, slots),
        (slots, SHARE),
        (slots, SHARE),
        (slots, BOTH),
        (slots, SHARE),
        (slots, BOTH + SHARE),
        (2, tokens, SHARE),
        (2, tokens, SHARE),
        None,
        (tokens, width),
        None,
        (2, 2, 2, tokens, pair),
        (2, 2, 2, tokens, pair),
        (4, tokens, SHARE),
        (4, tokens, SHARE),
    ]
    scratch = [
        pltpu.VMEM((2, tokens, SHARE), jnp.float32) if shape is None else pltpu.VMEM(shape, jnp.bfloat16)
        for shape in shapes
    ]
    counts = [4, 4] + [2 * experts] * 2 + [slots // GROUP] * 2 + [slots // BLOCK] * 2 + [2 * experts] * 2
    counts += [2] * 8 + [4] * 2
    return pl.pallas_call(
        layer_kernel,
        out_shape=[jax.ShapeDtypeStruct((tokens, half), jnp.bfloat16)] * 2,
        in_specs=[vmem] * 7 + [pl.BlockSpec(memory_space=pl.ANY)] * 4,
        out_specs=[vmem] * 2,
        scratch_shapes=scratch + [dma((count,)) for count in counts],
        compiler_params=pltpu.CompilerParams(
            collective_id=0, has_side_effects=True, vmem_limit_bytes=60 * 1024 * 1024
        ),
        cost_estimate=pl.CostEstimate(
            flops=4 * slots * width * inner, bytes_accessed=24 * 1024 * 1024, transcendentals=131072
        ),
        name="whole_layer",
    )(
        hidden,
        gain,
        router,
        routes,
        routes.T,
        src_row,
        tgt_column,
        first,
        second,
        weight,
        cotangent,
    )


def per_device(
    hidden_in,
    norm_gain,
    router,
    routes,
    expert_in,
    expert_out,
    attn_weight,
    src_segments,
    tgt_segments,
    cotangent,
):
    forward, backward = whole_layer(
        hidden_in[0],
        norm_gain,
        router[0],
        routes[0],
        src_segments,
        tgt_segments.reshape(-1, 1),
        expert_in[0, 0],
        expert_out[0, 0],
        attn_weight[0],
        cotangent,
    )
    return (forward[None], backward[None])


def solution(mesh):
    return jax.shard_map(
        per_device,
        mesh=mesh,
        in_specs=(
            P("grp", "dp", None),
            P("grp", None),
            P("grp", None, None),
            P("grp", "dp", None),
            P("grp", "dp", None, "mp"),
            P("grp", "dp", "mp", None),
            P("grp", None, None, "mp"),
            P("dp", None),
            P("dp", None),
            P("dp", None),
        ),
        out_specs=(P("grp", "dp", "mp"), P("grp", "dp", "mp")),
        check_vma=False,
    )
```

time: 173 us -> 153 us (0.88)
  Pallas kernels: 161 us -> 143 us
  local copies, waits for them, and re-layouts: 2.37 us -> 8.59 us
  other arithmetic: 4.68 us -> 0 us
  matrix products: 4.03 us -> 0 us
    pallas_call x2 -> x1, Pallas kernels: 161 us -> 143 us  [whole_layer(): pl.pallas_call(layer_kernel, out_shape=[jax.ShapeDtypeStruct((tokens, hal...]
    dot_general x3 -> x0, matrix products: 4.03 us -> none  [the longest x1 3.37 us: per_device(): lax.dot_general(places.any(1).astype(jnp.bfloat16), normed, (((0,), (0,))...]
    reduce_sum x5 -> x0, other arithmetic: 3.43 us -> none  [the longest x1 1.64 us: layer_norm(): variance = jnp.mean(centred * centred, -1, keepdims=True)]
    unnamed x14 -> x3, local copies, waits for them, and re-layouts: 2.23 us -> 5.64 us
where the time goes in v4:
time: 153 us; the launch traced here: 152 us
  Pallas kernels  143 us (93%)
  local copies, waits for them, and re-layouts  8.59 us (6%)
    pallas_call x1, Pallas kernels, whole_layer(): pl.pallas_call(layer_kernel, out_shape=[jax.ShapeDtypeStruct((tokens, hal...  143 us
    unnamed x3, local copies, waits for them, and re-layouts  5.64 us

profile of v4, /device:TPU:1, one launch (start us, length us, event | category | flops | bytes accessed | tf_op | source)
XLA Modules:
  0.0 152.2 jit_solution(14792732282111411329)
XLA Ops:
  0.6 1.5 copy.16.tgt_column
  2.1 1.5 copy.15.routes
  3.6 1.9 %copy.14 = bf16[1,2048,32]{2,1,0:T(8,128)(2,1)} copy(bf16[1,2048,32]{1,2,0:T(8,128)(2,1)} %param.12) | data formatting | bytes 262144 | tf_op args[2]
  5.5 143.0 %whole_layer.1 = (bf16[256,1024]{1,0:T(8,128)(2,1)}, bf16[256,1024]{1,0:T(8,128)(2,1)}) custom-call(bf16[256,2048]{1,0:T(8,128)(2,1)} %bitcast.20, bf16[1,2048]{1,0:T(2,128)(2,1)} %gain.1, bf16[2048,32]{1,0:T(8,128)(2,1)} %bitcast.11, s32[256,2]{1,0:T(8,128)} %copy.15.routes, s32[2,256]{1,0:T(2,128)} %bitcast.15, s32[1,256]{1,0:T(1,128)} %src_row.1, ...), custom_call_target="tpu_custom_call" | custom-call | flops 17179869184 | bytes 25165824 | tf_op jit(solution)/shard_map/whole_layer/pallas_call | solution.py:540
  148.5 1.9 %copy.19 = bf16[1,256,1024]{2,1,0:T(8,128)(2,1)} copy(bf16[1,256,1024]{2,1,0:T(8,128)(2,1)} %bitcast.13) | data formatting | bytes 1048576
  150.4 1.9 %copy.20 = bf16[1,256,1024]{2,1,0:T(8,128)(2,1)} copy(bf16[1,256,1024]{2,1,0:T(8,128)(2,1)} %bitcast.12) | data formatting | bytes 1048576

commit v5 on v4

--- a/solution.py
+++ b/solution.py
@@ -11,6 +11,7 @@
 RINGS = (2, 4, 4)
 SHARE = 512
 BOTH = 1024
+LATE = 256
 GROUP = 128
 BLOCK = 256
 TILE = 256
@@ -55,11 +56,10 @@
 def layer_kernel(
     hidden,
     gain,
-    router,
-    routes,
+    router_t,
     routes_t,
     src_row,
-    tgt_column,
+    tgt_row,
     first_hbm,
     second_hbm,
     weight_hbm,
@@ -76,6 +76,7 @@
     cotangent,
     coarse,
     fine,
+    match_rows,
     for_partner,
     from_partner,
     both,
@@ -83,7 +84,6 @@
     returned,
     mix_out,
     mix_in,
-    own_mix,
     state,
     projected,
     held,
@@ -220,22 +220,23 @@
     for slot in range(experts):
         send(slot, 1)
 
-    named = [routes[:, k : k + 1] == iota((tokens, experts), 1) for k in range(2)]
-    earlier = jnp.dot(
-        ones_where(iota(square, 0) > iota(square, 1)).astype(jnp.bfloat16),
-        (ones_where(named[0]) + ones_where(named[1])).astype(jnp.bfloat16),
-        preferred_element_type=jnp.float32,
-    )
-    logits = jnp.dot(normed[...], router[...], preferred_element_type=jnp.float32)
+    logits_t = contract_rows(router_t[...], normed[...])
 
     def chosen_of(values, k):
-        return jnp.sum(jnp.where(named[k], values, 0.0), 1, keepdims=True)
-
-    leading = jax.nn.sigmoid(chosen_of(logits, 0) - chosen_of(logits, 1))
-    gates = (leading, 1.0 - leading)
-    spots = [routes[:, k : k + 1] * cap + chosen_of(earlier, k).astype(jnp.int32) for k in range(2)]
+        return jnp.sum(jnp.where(named_t[k], values, 0.0), 0, keepdims=True)
+
+    def spot_of(k):
+        return routes_t[k : k + 1, :].astype(jnp.float32) * cap + rank_t[k]
+
+    leading_t = jax.nn.sigmoid(chosen_of(logits_t, 0) - chosen_of(logits_t, 1))
+    rows_t = [spot_of(0), spot_of(1), leading_t, tgt_row[...].astype(jnp.float32)]
+    token_columns = jnp.concatenate(rows_t + [jnp.zeros((4, tokens), jnp.float32)], 0).T
+    spots = (token_columns[:, 0:1], token_columns[:, 1:2])
+    gates = (token_columns[:, 2:3], 1.0 - token_columns[:, 2:3])
+    matches = token_columns[:, 3:4] == src_row[...].astype(jnp.float32)
+    match_rows[...] = ones_where(matches)
     for start in range(0, slots, BLOCK):
-        columns = iota((tokens, BLOCK), 1) + start
+        columns = (iota((tokens, BLOCK), 1) + start).astype(jnp.float32)
         mixing = jnp.where(spots[0] == columns, gates[0], 0.0) + jnp.where(spots[1] == columns, gates[1], 0.0)
         rough = mixing.astype(jnp.bfloat16)
         coarse[:, start : start + BLOCK] = rough
@@ -272,23 +273,41 @@
     def _():
         projected[1] = project(cotangent, 1, pl.ds(0, width))
 
-    def up_project(block):
+    def tiles(count, step):
+        def run(tile, carry):
+            step(pl.ds(pl.multiple_of(tile * TILE, TILE), TILE))
+            return carry
+
+        lax.fori_loop(0, count // TILE, run, 0)
+
+    def up_shared(block):
         rows = pl.ds(block * BLOCK, BLOCK)
 
-        def step(tile, carry):
-            columns = pl.ds(pl.multiple_of(tile * TILE, TILE), TILE)
-            product = jnp.dot(arrived[rows, :], first[:, columns], preferred_element_type=jnp.float32)
-            inner[rows, columns] = jnp.maximum(product, 0.0).astype(jnp.bfloat16)
-            return carry
-
-        lax.fori_loop(0, inner.shape[1] // TILE, step, 0)
+        def step(columns):
+            product = jnp.dot(
+                arrived[rows, :SHARE], first[:SHARE, columns], preferred_element_type=jnp.float32
+            ) + jnp.dot(
+                arrived[rows, SHARE + BOTH :], first[SHARE + BOTH :, columns], preferred_element_type=jnp.float32
+            )
+            inner[rows, columns] = product.astype(jnp.bfloat16)
+
+        tiles(inner.shape[1], step)
+
+    def up_rest(block):
+        rows = pl.ds(block * BLOCK, BLOCK)
+        middle = pl.ds(SHARE, BOTH)
+
+        def step(columns):
+            product = jnp.dot(arrived[rows, middle], first[middle, columns], preferred_element_type=jnp.float32)
+            total = product + inner[rows, columns].astype(jnp.float32)
+            inner[rows, columns] = jnp.maximum(total, 0.0).astype(jnp.bfloat16)
+
+        tiles(inner.shape[1], step)
 
     for block in range(blocks):
         for number in range(block * BLOCK // GROUP, (block + 1) * BLOCK // GROUP):
             pass_on(number, their_start).wait_recv()
-        for slot in range(block * per_block, (block + 1) * per_block):
-            wait_arrival(slot, 1)
-        up_project(block)
+        up_shared(block)
 
     def down_project(block, start, count, finish):
         rows = pl.ds(block * BLOCK, BLOCK)
@@ -316,8 +335,9 @@
         return remote(for_partner.at[rows], from_partner.at[rows], half_sem.at[block], halved_sem.at[block], partner)
 
     def give_back(slot, part, expert, where):
-        buffer, start, count = ((both, 0, BOTH), (share, BOTH, SHARE))[part]
-        source = buffer.at[pl.ds(slot * cap, cap)]
+        start, count = (0, BOTH) if part == 0 else (BOTH + (part - 1) * LATE, LATE)
+        rows = pl.ds(slot * cap, cap)
+        source = both.at[rows] if part == 0 else share.at[rows, pl.ds(start - BOTH, LATE)]
         target = returned.at[pl.ds(pl.multiple_of(expert * cap, cap), cap), pl.ds(start, count)]
         if slot == 0:
             return pltpu.make_async_copy(source, target, own_sem.at[2 + part])
@@ -334,15 +354,19 @@
     loads[3].wait()
     halves = [halve(block) for block in range(blocks)]
     for block in range(blocks):
+        for slot in range(block * per_block, (block + 1) * per_block):
+            wait_arrival(slot, 1)
+        up_rest(block)
+        down_project(block, SHARE, BOTH, keep_in(both))
+        give_block_back(block, 0)
         down_project(block, their_start, SHARE, keep_in(for_partner))
         halves[block].start()
-    for block in range(blocks):
-        down_project(block, SHARE, BOTH, keep_in(both))
-        give_block_back(block, 0)
     for block in range(blocks):
         halves[block].wait_recv()
         down_project(block, own_start, SHARE, add_share)
         give_block_back(block, 1)
+    for block in range(blocks):
+        give_block_back(block, 2)
 
     def mix_rows(rows, columns):
         values = returned[rows, columns]
@@ -354,21 +378,27 @@
         if part == 0:
             return mix_rows(pl.ds(0, slots), span((mp if mine else 1 - mp) * SHARE))
         which = row_h if mine else 1 - row_h
-        return mix_rows(span(which * (slots // 2), slots // 2), pl.ds(BOTH, SHARE))
+        return mix_rows(span(which * (slots // 2), slots // 2), pl.ds(BOTH + (part - 1) * LATE, LATE))
 
     def piece(part, side):
-        return span(SHARE + side * SHARE) if part == 0 else span(side * (SHARE + BOTH))
-
+        if part == 0:
+            return span(SHARE + side * SHARE)
+        return pl.ds(pl.multiple_of(side * (SHARE + BOTH) + (part - 1) * LATE, LATE), LATE)
+
+    parts = 1 + SHARE // LATE
+    mix_columns = [pl.ds(0, SHARE)] + [pl.ds(SHARE + late * LATE, LATE) for late in range(parts - 1)]
     mixes = [
-        remote(mix_out.at[part], mix_in.at[part], mix_sent.at[part], mix_here.at[part], partner)
-        for part in range(2)
+        remote(
+            mix_out.at[:, columns], mix_in.at[:, columns], mix_sent.at[part], mix_here.at[part], partner
+        )
+        for part, columns in enumerate(mix_columns)
     ]
 
     def hand_state(part, side):
         region = state.at[:, piece(part, side)]
         return remote(region, region, state_sent.at[part], state_here.at[part], partner)
 
-    hands = [hand_state(part, mp) for part in range(2)]
+    hands = [hand_state(part, mp) for part in range(parts)]
 
     def project_piece(part, side, opening):
         columns = piece(part, side)
@@ -380,24 +410,24 @@
             other = project(state, 1, columns)
             projected[1] = other if opening else projected[1] + other
 
-    for part in range(2):
+    for part in range(parts):
         for slot in range(experts):
             if slot > 0:
                 give_back(slot, part, place(OFFSETS[slot], 1)[0], partner).wait_recv()
             else:
                 backs[part * experts][2].wait()
-        mix_out[part] = mix_part(part, False).astype(jnp.bfloat16)
+        mix_out[:, mix_columns[part]] = mix_part(part, False).astype(jnp.bfloat16)
         mixes[part].start()
-        own_mix[part] = mix_part(part, True)
+        own = mix_part(part, True)
         mixes[part].wait_recv()
         columns = piece(part, mp)
         total = hidden[:, columns].astype(jnp.float32) + (
-            own_mix[part] + mix_in[part].astype(jnp.float32)
+            own + mix_in[:, mix_columns[part]].astype(jnp.float32)
         )
         state[:, columns] = total.astype(jnp.bfloat16)
         hands[part].start()
         project_piece(part, mp, part == 0)
-    for part in range(2):
+    for part in range(parts):
         hand_state(part, 1 - mp).wait_recv()
         project_piece(part, 1 - mp, False)
 
@@ -415,7 +445,7 @@
     handed = [hand_held(which, group, 1 - group) for which in range(2)]
     for which in range(2):
         handed[which].start()
-    matches = tgt_column[...] == src_row[...]
+    matches = match_rows[...] > 0.0
     for which in range(2):
         hand_held(which, 1 - group, group).wait_recv()
 
@@ -497,7 +527,7 @@
         copy.wait_send()
 
 
-def whole_layer(hidden, gain, router, routes, src_row, tgt_column, first, second, weight, cotangent):
+def whole_layer(hidden, gain, router, routes, src_row, tgt_row, first, second, weight, cotangent):
     tokens, width = hidden.shape
     half, inner = width // 2, first.shape[1]
     experts = router.shape[1]
@@ -516,31 +546,34 @@
         cotangent.shape,
         (tokens, slots),
         (tokens, slots),
+        (tokens, tokens, jnp.float32),
         (slots, SHARE),
         (slots, SHARE),
         (slots, BOTH),
         (slots, SHARE),
         (slots, BOTH + SHARE),
-        (2, tokens, SHARE),
-        (2, tokens, SHARE),
-        None,
+        (tokens, 2 * SHARE),
+        (tokens, 2 * SHARE),
         (tokens, width),
-        None,
+        (2, tokens, 2 * pair, jnp.float32),
         (2, 2, 2, tokens, pair),
         (2, 2, 2, tokens, pair),
         (4, tokens, SHARE),
         (4, tokens, SHARE),
     ]
     scratch = [
-        pltpu.VMEM((2, tokens, SHARE), jnp.float32) if shape is None else pltpu.VMEM(shape, jnp.bfloat16)
+        pltpu.VMEM(shape[:-1], shape[-1])
+        if shape[-1] is jnp.float32
+        else pltpu.VMEM(shape, jnp.bfloat16)
         for shape in shapes
     ]
-    counts = [4, 4] + [2 * experts] * 2 + [slots // GROUP] * 2 + [slots // BLOCK] * 2 + [2 * experts] * 2
-    counts += [2] * 8 + [4] * 2
+    parts = 1 + SHARE // LATE
+    counts = [4, 2 + parts] + [2 * experts] * 2 + [slots // GROUP] * 2 + [slots // BLOCK] * 2
+    counts += [parts * experts] * 2 + [parts] * 4 + [2] * 4 + [4] * 2
     return pl.pallas_call(
         layer_kernel,
         out_shape=[jax.ShapeDtypeStruct((tokens, half), jnp.bfloat16)] * 2,
-        in_specs=[vmem] * 7 + [pl.BlockSpec(memory_space=pl.ANY)] * 4,
+        in_specs=[vmem] * 6 + [pl.BlockSpec(memory_space=pl.ANY)] * 4,
         out_specs=[vmem] * 2,
         scratch_shapes=scratch + [dma((count,)) for count in counts],
         compiler_params=pltpu.CompilerParams(
@@ -553,11 +586,10 @@
     )(
         hidden,
         gain,
-        router,
-        routes,
+        router.T,
         routes.T,
         src_row,
-        tgt_column,
+        tgt_row,
         first,
         second,
         weight,
@@ -583,7 +615,7 @@
         router[0],
         routes[0],
         src_segments,
-        tgt_segments.reshape(-1, 1),
+        tgt_segments,
         expert_in[0, 0],
         expert_out[0, 0],
         attn_weight[0],

time: 153 us -> 138 us (0.902)
  Pallas kernels: 143 us -> 132 us
  local copies, waits for them, and re-layouts: 8.59 us -> 3.74 us
    pallas_call x1, Pallas kernels: 143 us -> 132 us  [whole_layer(): pl.pallas_call(layer_kernel, out_shape=[jax.ShapeDtypeStruct((tokens, hal...]
    unnamed x3 -> x2, local copies, waits for them, and re-layouts: 5.64 us -> 3.74 us
where the time goes in v5:
time: 138 us; the launch traced here: 137 us
  Pallas kernels  132 us (96%)
  local copies, waits for them, and re-layouts  3.74 us (3%)
    pallas_call x1, Pallas kernels, whole_layer(): pl.pallas_call(layer_kernel, out_shape=[jax.ShapeDtypeStruct((tokens, hal...  132 us
    unnamed x2, local copies, waits for them, and re-layouts  3.74 us

profile of v5, /device:TPU:1, one launch (start us, length us, event | category | flops | bytes accessed | tf_op | source)
XLA Modules:
  0.0 136.7 jit_solution(16090305308268002618)
XLA Ops:
  0.6 132.3 %whole_layer.1 = (bf16[256,1024]{1,0:T(8,128)(2,1)}, bf16[256,1024]{1,0:T(8,128)(2,1)}) custom-call(bf16[256,2048]{1,0:T(8,128)(2,1)} %bitcast.17, bf16[1,2048]{1,0:T(2,128)(2,1)} %gain.1, bf16[32,2048]{1,0:T(8,128)(2,1)} %bitcast.18, s32[2,256]{1,0:T(2,128)} %bitcast.19, s32[1,256]{1,0:T(1,128)} %src_row.1, s32[1,256]{1,0:T(1,128)} %tgt_row.1, ...), custom_call_target="tpu_custom_call" | custom-call | flops 17179869184 | bytes 25165824 | tf_op jit(solution)/shard_map/whole_layer/pallas_call | solution.py:573
  132.9 1.9 %copy.14 = bf16[1,256,1024]{2,1,0:T(8,128)(2,1)} copy(bf16[1,256,1024]{2,1,0:T(8,128)(2,1)} %bitcast.13) | data formatting | bytes 1048576
  134.8 1.9 %copy.15 = bf16[1,256,1024]{2,1,0:T(8,128)(2,1)} copy(bf16[1,256,1024]{2,1,0:T(8,128)(2,1)} %bitcast.12) | data formatting | bytes 1048576

commit v6 on v5

--- a/solution.py
+++ b/solution.py
@@ -90,6 +90,8 @@
     grads,
     final_out,
     final_in,
+    ahead,
+    gathered,
     load_sem,
     own_sem,
     send_sem,
@@ -110,6 +112,10 @@
     grad_here,
     final_sent,
     final_here,
+    ahead_sent,
+    ahead_here,
+    gather_sent,
+    gather_here,
 ):
     group, row, mp = lax.axis_index("grp"), lax.axis_index("dp"), lax.axis_index("mp")
     experts = len(OFFSETS)
@@ -119,6 +125,8 @@
     half = width // 2
     row_h, row_z, row_y = row // 16, row // 4 % 4, row % 4
     partner, core = {"mp": 1 - mp}, {"grp": 1 - group}
+    across = {"grp": 1 - group, "mp": 1 - mp}
+    decoder_across = {"grp": 1, "mp": 1 - mp}
 
     def place(offset, sign):
         dh, dz, dy = offset
@@ -139,7 +147,7 @@
         return pl.ds(pl.multiple_of(start, SHARE), count)
 
     barrier = pltpu.get_barrier_semaphore()
-    greeted = [device(*place(offset, -1)) for offset in OFFSETS[1:]] + [partner, core]
+    greeted = [device(*place(offset, -1)) for offset in OFFSETS[1:]] + [partner, core, across]
     for where in greeted:
         pl.semaphore_signal(barrier, inc=1, device_id=where, device_id_type=pl.DeviceIdType.MESH)
     loads = [
@@ -148,8 +156,6 @@
             ((first_hbm, first), (weight_hbm, weight), (cotangent_hbm, cotangent), (second_hbm, second))
         )
     ]
-    for load in loads:
-        load.start()
 
     norm_rows = 64
 
@@ -202,6 +208,10 @@
         index, side = place(OFFSETS[slot], 1)
         sends.append((slot, part, dispatch(slot, part, side, device(index, side))))
         sends[-1][2].start()
+
+    def send_ahead(which, side):
+        source = weight_hbm.at[which, span(side * half, half)]
+        return remote(source, ahead.at[which], ahead_sent.at[which], ahead_here.at[which], partner)
 
     blocks = slots // BLOCK
     per_block = BLOCK // cap
@@ -215,10 +225,17 @@
             ).astype(jnp.bfloat16)
         if block == 0:
             pl.semaphore_wait(barrier, len(greeted))
+
+            @pl.when(group == 1)
+            def _():
+                send_ahead(0, 1 - mp).start()
+
         for slot in range(block * per_block, (block + 1) * per_block):
             send(slot, 0)
     for slot in range(experts):
         send(slot, 1)
+    for load in loads:
+        load.start()
 
     logits_t = contract_rows(router_t[...], normed[...])
 
@@ -262,6 +279,10 @@
         for slot in range(number * per_group, (number + 1) * per_group):
             wait_arrival(slot, 0)
         passes[number].start()
+
+    @pl.when(group == 1)
+    def _():
+        send_ahead(1, 1 - mp).start()
 
     def project(source, which, columns):
         return jnp.dot(source[:, columns], weight[which, columns, :], preferred_element_type=jnp.float32)
@@ -468,6 +489,20 @@
     given = [hand_grad(which, 1 - group, group) for which in range(2)]
     for which in range(2):
         given[which].start()
+
+    def gather(which, heads):
+        number = which * 2 + heads
+        return remote(
+            grads.at[1, which, heads],
+            gathered.at[which, heads],
+            gather_sent.at[which],
+            gather_here.at[number],
+            decoder_across,
+        )
+
+    gathers = [gather(which, group) for which in range(2)]
+    for which in range(2):
+        gathers[which].start()
     for which in range(2):
         hand_grad(which, group, 1 - group).wait_recv()
 
@@ -489,41 +524,39 @@
             start = (1 - mp) * half + chunk * SHARE
             final_out[chunk] = (back_project(0, start) + back_project(1, start)).astype(jnp.bfloat16)
             final(0, chunk).start()
-        forward[...] = state[:, span(mp * half, half)]
+        forward[...] = state[:, span(mp * half, half)].astype(jnp.float32)
         for chunk in range(2):
             start = mp * half + chunk * SHARE
             own = back_project(0, start) + back_project(1, start)
             final(0, chunk).wait_recv()
             backward[:, chunk * SHARE : (chunk + 1) * SHARE] = (
                 own + final_in[chunk].astype(jnp.float32)
-            ).astype(jnp.bfloat16)
+            )
         for chunk in range(2):
             final(0, chunk).wait_send()
 
     @pl.when(group == 1)
     def _():
         for which in range(2):
+            send_ahead(which, mp).wait_recv()
+        for which, base, target in ((0, cotangent, backward), (1, state, forward)):
+            own = [back_project(which, mp * half + chunk * SHARE) for chunk in range(2)]
+            for heads in range(2):
+                gather(which, heads).wait_recv()
             for chunk in range(2):
-                start = (1 - mp) * half + chunk * SHARE
-                final_out[which * 2 + chunk] = back_project(which, start).astype(jnp.bfloat16)
-                final(which, chunk).start()
-        for which, base, target in ((0, cotangent, backward), (1, state, forward)):
-            for chunk in range(2):
-                start = mp * half + chunk * SHARE
-                own = back_project(which, start)
-                final(which, chunk).wait_recv()
-                total = base[:, span(start)].astype(jnp.float32) + (
-                    own + final_in[which * 2 + chunk].astype(jnp.float32)
+                rows = pl.ds(chunk * SHARE, SHARE)
+                theirs = contract_rows(gathered[which, 0], ahead[which, rows, :pair]) + contract_rows(
+                    gathered[which, 1], ahead[which, rows, pair:]
                 )
-                target[:, chunk * SHARE : (chunk + 1) * SHARE] = total.astype(jnp.bfloat16)
+                total = base[:, span(mp * half + chunk * SHARE)].astype(jnp.float32) + (own[chunk] + theirs)
+                target[:, chunk * SHARE : (chunk + 1) * SHARE] = total
         for which in range(2):
-            for chunk in range(2):
-                final(which, chunk).wait_send()
+            send_ahead(which, 1 - mp).wait_send()
 
     for slot, part, copy in sends + backs:
         if slot > 0:
             copy.wait_send()
-    for copy in passes + halves + mixes + hands + handed + given:
+    for copy in passes + halves + mixes + hands + handed + given + gathers:
         copy.wait_send()
 
 
@@ -558,8 +591,10 @@
         (2, tokens, 2 * pair, jnp.float32),
         (2, 2, 2, tokens, pair),
         (2, 2, 2, tokens, pair),
-        (4, tokens, SHARE),
-        (4, tokens, SHARE),
+        (2, tokens, SHARE),
+        (2, tokens, SHARE),
+        (2, half, 2 * pair),
+        (2, 2, tokens, pair),
     ]
     scratch = [
         pltpu.VMEM(shape[:-1], shape[-1])
@@ -569,10 +604,10 @@
     ]
     parts = 1 + SHARE // LATE
     counts = [4, 2 + parts] + [2 * experts] * 2 + [slots // GROUP] * 2 + [slots // BLOCK] * 2
-    counts += [parts * experts] * 2 + [parts] * 4 + [2] * 4 + [4] * 2
+    counts += [parts * experts] * 2 + [parts] * 4 + [2] * 4 + [2] * 2 + [2] * 3 + [4]
     return pl.pallas_call(
         layer_kernel,
-        out_shape=[jax.ShapeDtypeStruct((tokens, half), jnp.bfloat16)] * 2,
+        out_shape=[jax.ShapeDtypeStruct((tokens, half), jnp.float32)] * 2,
         in_specs=[vmem] * 6 + [pl.BlockSpec(memory_space=pl.ANY)] * 4,
         out_specs=[vmem] * 2,
         scratch_shapes=scratch + [dma((count,)) for count in counts],
@@ -621,7 +656,7 @@
         attn_weight[0],
         cotangent,
     )
-    return (forward[None], backward[None])
+    return (forward.astype(jnp.bfloat16)[None], backward.astype(jnp.bfloat16)[None])
 
 
 def solution(mesh):

time: 138 us -> 134 us (0.971)
  the two profiles are of different devices: /device:TPU:1 before, /device:TPU:8 now
where the time goes in v6:
time: 134 us
  Pallas kernels  130 us (97%)
  other arithmetic  2.67 us (2%)
    pallas_call x1, Pallas kernels, whole_layer(): pl.pallas_call(layer_kernel, out_shape=[jax.ShapeDtypeStruct((tokens, hal...  130 us

profile of v6, /device:TPU:8, one launch (start us, length us, event | category | flops | bytes accessed | tf_op | source)
XLA Modules:
  0.0 133.6 jit_solution(2303939580343160712)
XLA Ops:
  0.6 130.3 %whole_layer.1 = (f32[256,1024]{1,0:T(8,128)}, f32[256,1024]{1,0:T(8,128)}) custom-call(bf16[256,2048]{1,0:T(8,128)(2,1)} %bitcast.17, bf16[1,2048]{1,0:T(2,128)(2,1)} %gain.1, bf16[32,2048]{1,0:T(8,128)(2,1)} %bitcast.18, s32[2,256]{1,0:T(2,128)} %bitcast.19, s32[1,256]{1,0:T(1,128)} %src_row.1, s32[1,256]{1,0:T(1,128)} %tgt_row.1, ...), custom_call_target="tpu_custom_call" | custom-call | flops 17179869184 | bytes 25165824 | tf_op jit(solution)/shard_map/whole_layer/pallas_call | solution.py:608
  130.9 2.7 %convert_bitcast_fusion = (bf16[1,256,1024]{2,1,0:T(8,128)(2,1)}, bf16[1,256,1024]{2,1,0:T(8,128)(2,1)}) fusion(f32[256,1024]{1,0:T(8,128)} %get-tuple-element.5, f32[256,1024]{1,0:T(8,128)} %get-tuple-element.4), kind=kLoop, calls=%fused_computation | loop fusion | flops 524288 | bytes 3145728 | tf_op jit(solution)/shard_map/broadcast_in_dim | solution.py:659

commit v7 on v6

--- a/solution.py
+++ b/solution.py
@@ -431,7 +431,7 @@
             other = project(state, 1, columns)
             projected[1] = other if opening else projected[1] + other
 
-    for part in range(parts):
+    def open_part(part):
         for slot in range(experts):
             if slot > 0:
                 give_back(slot, part, place(OFFSETS[slot], 1)[0], partner).wait_recv()
@@ -439,7 +439,9 @@
                 backs[part * experts][2].wait()
         mix_out[:, mix_columns[part]] = mix_part(part, False).astype(jnp.bfloat16)
         mixes[part].start()
-        own = mix_part(part, True)
+        return mix_part(part, True)
+
+    def close_part(part, own):
         mixes[part].wait_recv()
         columns = piece(part, mp)
         total = hidden[:, columns].astype(jnp.float32) + (
@@ -447,7 +449,15 @@
         )
         state[:, columns] = total.astype(jnp.bfloat16)
         hands[part].start()
-        project_piece(part, mp, part == 0)
+
+    opened = open_part(0)
+    for part in range(parts):
+        if part > 0:
+            project_piece(part - 1, mp, part == 1)
+        following = open_part(part + 1) if part > 0 and part + 1 < parts else None
+        close_part(part, opened)
+        opened = following if part > 0 else open_part(1)
+    project_piece(parts - 1, mp, False)
     for part in range(parts):
         hand_state(part, 1 - mp).wait_recv()
         project_piece(part, 1 - mp, False)

time: 134 us -> 131 us (0.978)
  Pallas kernels: 130 us -> 127 us
    pallas_call x1, Pallas kernels: 130 us -> 127 us  [whole_layer(): pl.pallas_call(layer_kernel, out_shape=[jax.ShapeDtypeStruct((tokens, hal...]
where the time goes in v7:
time: 131 us
  Pallas kernels  127 us (97%)
  other arithmetic  2.67 us (2%)
    pallas_call x1, Pallas kernels, whole_layer(): pl.pallas_call(layer_kernel, out_shape=[jax.ShapeDtypeStruct((tokens, hal...  127 us
    broadcast_in_dim x1, other arithmetic, per_device(): backward.astype(jnp.bfloat16)[None]  2.67 us

profile of v7, /device:TPU:8, one launch (start us, length us, event | category | flops | bytes accessed | tf_op | source)
XLA Modules:
  0.0 130.7 jit_solution(8810614200857894821)
XLA Ops:
  0.6 127.4 %whole_layer.1 = (f32[256,1024]{1,0:T(8,128)}, f32[256,1024]{1,0:T(8,128)}) custom-call(bf16[256,2048]{1,0:T(8,128)(2,1)} %bitcast.17, bf16[1,2048]{1,0:T(2,128)(2,1)} %gain.1, bf16[32,2048]{1,0:T(8,128)(2,1)} %bitcast.18, s32[2,256]{1,0:T(2,128)} %bitcast.19, s32[1,256]{1,0:T(1,128)} %src_row.1, s32[1,256]{1,0:T(1,128)} %tgt_row.1, ...), custom_call_target="tpu_custom_call" | custom-call | flops 17179869184 | bytes 25165824 | tf_op jit(solution)/shard_map/whole_layer/pallas_call | solution.py:618
  128.0 2.7 %convert_bitcast_fusion = (bf16[1,256,1024]{2,1,0:T(8,128)(2,1)}, bf16[1,256,1024]{2,1,0:T(8,128)(2,1)}) fusion(f32[256,1024]{1,0:T(8,128)} %get-tuple-element.5, f32[256,1024]{1,0:T(8,128)} %get-tuple-element.4), kind=kLoop, calls=%fused_computation | loop fusion | flops 524288 | bytes 3145728 | tf_op jit(solution)/shard_map/broadcast_in_dim | solution.py:669
